TPU v7x, 32 devices: a whole 2x2x4 slice. The times are simulated.
32 devices in a mesh: seq: 8 (over y, x, core), batch: 4 (over z).
Axes of the slice: x: 2, y: 2, z: 4, core: 2. Of those that a mesh axis runs over, the one named last changes fastest.
Arguments:
- inputs: bfloat16 [4, 3072, 512], P('batch', 'seq'), may hold values from -6 to 6
- memory: bfloat16 [4, 1536, 512], P('batch', 'seq'), may hold values from -6 to 6
- target_lengths: int32 [4, 33], P('batch'), may hold values from 32 to 1024, as said below
- source_lengths: int32 [4, 33], P('batch'), may hold values from 16 to 512, as said below
- target_order: int32 [4, 16], P('batch'), may hold values from 0 to 15, as said below
- source_order: int32 [4, 16], P('batch'), may hold values from 0 to 15, as said below
- self_gain: bfloat16 [512], replicated, may hold values from 0.099609375 to 1.8984375
- self_shift: bfloat16 [512], replicated, may hold values from -1.75 to 1.75
- self_query: bfloat16 [512, 512], replicated, may hold values from -0.25 to 0.25
- query_bias: bfloat16 [512], replicated, may hold values from -1.75 to 1.75
- self_key: bfloat16 [512, 512], replicated, may hold values from -0.25 to 0.25
- self_value: bfloat16 [512, 512], replicated, may hold values from -0.25 to 0.25
- value_bias: bfloat16 [512], replicated, may hold values from -1.75 to 1.75
- self_output: bfloat16 [512, 512], replicated, may hold values from -1 to 1
- output_bias: bfloat16 [512], replicated, may hold values from -1.75 to 1.75
- cross_gain: bfloat16 [512], replicated, may hold values from 0.099609375 to 1.8984375
- cross_shift: bfloat16 [512], replicated, may hold values from -1.75 to 1.75
- cross_query: bfloat16 [512, 512], replicated, may hold values from -0.25 to 0.25
- cquery_bias: bfloat16 [512], replicated, may hold values from -1.75 to 1.75
- cross_key: bfloat16 [512, 512], replicated, may hold values from -0.25 to 0.25
- cross_value: bfloat16 [512, 512], replicated, may hold values from -0.25 to 0.25
- cvalue_bias: bfloat16 [512], replicated, may hold values from -1.75 to 1.75
- cross_output: bfloat16 [512, 512], replicated, may hold values from -1 to 1
- coutput_bias: bfloat16 [512], replicated, may hold values from -1.75 to 1.75
- final_gain: bfloat16 [512], replicated, may hold values from 0.099609375 to 1.8984375
- final_shift: bfloat16 [512], replicated, may hold values from -1.75 to 1.75
- inner_weight: bfloat16 [512, 2048], replicated, may hold values from -0.25 to 0.25
- inner_bias: bfloat16 [2048], replicated, may hold values from -1.75 to 1.75
- outer_weight: bfloat16 [2048, 512], replicated, may hold values from -0.125 to 0.125
- outer_bias: bfloat16 [512], replicated, may hold values from -1.75 to 1.75
- cotangent: bfloat16 [4, 3072, 512], P('batch', 'seq'), may hold values from -6 to 6
Outputs:
- block_output: bfloat16 [4, 3072, 512], P('batch', 'seq')
- inputs_grad: float32 [4, 3072, 512], P('batch', 'seq')
- memory_grad: float32 [4, 1536, 512], P('batch', 'seq')
- self_gain_grad: float32 [512], replicated
- self_shift_grad: float32 [512], replicated
- self_query_grad: float32 [512, 512], replicated
- query_bias_grad: float32 [512], replicated
- self_key_grad: float32 [512, 512], replicated
- self_value_grad: float32 [512, 512], replicated
- value_bias_grad: float32 [512], replicated
- self_output_grad: float32 [512, 512], replicated
- output_bias_grad: float32 [512], replicated
- cross_gain_grad: float32 [512], replicated
- cross_shift_grad: float32 [512], replicated
- cross_query_grad: float32 [512, 512], replicated
- cquery_bias_grad: float32 [512], replicated
- cross_key_grad: float32 [512, 512], replicated
- cross_value_grad: float32 [512, 512], replicated
- cvalue_bias_grad: float32 [512], replicated
- cross_output_grad: float32 [512, 512], replicated
- coutput_bias_grad: float32 [512], replicated
- final_gain_grad: float32 [512], replicated
- final_shift_grad: float32 [512], replicated
- inner_weight_grad: float32 [512, 2048], replicated
- inner_bias_grad: float32 [2048], replicated
- outer_weight_grad: float32 [2048, 512], replicated
- outer_bias_grad: float32 [512], replicated
Inputs may be any that keep to these rules, and one draw needn't show every extreme that they name: `target_lengths`: in each stream exactly one document, at an index drawn from the seed, has 1024 target tokens; the others have 64//2 to 64; the lengths sum to at most 3072, and stream positions past the sum are padding. `source_lengths`: document d's source pairs with target document d; the document that has 1024 target tokens has exactly 512 source tokens, the others 32//2 to 31; the lengths sum to less than 1536, so the last source position is always padding. Each row is a permutation of 0 to 15: stored block s holds stream block target_order[s]. Each row is a permutation of 0 to 15: stored block s holds source stream block source_order[s].
All inputs are finite; a program needn't handle non-finite values.
Results may differ from a plain program's by a relative error of at most 0.025.
Values may be sent and summed in bfloat16 or wider, within the bound.
A program may use at most 448 MiB of HBM per device.

v0:
```python
import math

import jax
import jax.numpy as jnp
from jax import lax
from jax.sharding import PartitionSpec as P

D = 512
HEADS = 8


EPSILON = 1e-05
NEGATIVE = -1e30


def norm(values, gain, shift):
    center = values - jnp.mean(values, axis=-1, keepdims=True)
    spread = jnp.mean(center * center, axis=-1, keepdims=True)
    return center * lax.rsqrt(spread + EPSILON) * gain + shift


def product(left, right):
    return jnp.dot(left, right, preferred_element_type=jnp.float32)


def weight_grad(left, right):
    return jnp.einsum("ti,to->io", left, right, preferred_element_type=jnp.float32)


def input_grad(grad, weight):
    return jnp.einsum("to,io->ti", grad, weight, preferred_element_type=jnp.float32)


def split_heads(values):
    return values.reshape(values.shape[0], HEADS, -1)


def locate(order, lengths, blocksize, start, count):
    index = start + jnp.arange(count, dtype=jnp.int32)
    slot = index // blocksize
    picked = jnp.sum(
        jnp.where(
            slot[:, None] == jnp.arange(order.shape[0], dtype=jnp.int32)[None, :], order[None, :], 0
        ),
        axis=1,
    )
    position = picked * blocksize + index % blocksize
    ends = jnp.cumsum(lengths)
    document = jnp.sum((position[:, None] >= ends[None, :]).astype(jnp.int32), axis=1)
    return (document, position)


def visible(query_doc, query_pos, key_doc, key_pos, causal):
    same = query_doc[:, None] == key_doc[None, :]
    if causal:
        return same & (key_pos[None, :] <= query_pos[:, None])
    return same


def opening(rows):
    return (
        jnp.zeros((rows, HEADS, D // HEADS), jnp.float32),
        jnp.full((rows, HEADS), NEGATIVE, jnp.float32),
        jnp.zeros((rows, HEADS), jnp.float32),
    )


def online(carry, query_heads, piece_keys, piece_values, allowed):
    weighted, highest, total = carry
    scores = jnp.einsum(
        "qhd,khd->qhk", query_heads, split_heads(piece_keys), preferred_element_type=jnp.float32
    )
    allowed = allowed[:, None, :]
    raised = jnp.maximum(highest, jnp.max(jnp.where(allowed, scores, NEGATIVE), axis=-1))
    powers = jnp.exp(jnp.where(allowed, scores - raised[..., None], NEGATIVE))
    total = jnp.sum(powers, axis=-1)
    weighted = jnp.einsum(
        "qhk,khd->qhd",
        powers.astype(jnp.bfloat16),
        split_heads(piece_values),
        preferred_element_type=jnp.float32,
    )
    return (weighted, raised, total)


def finish(carry):
    weighted, highest, total = carry
    return (highest + jnp.log(total), (weighted / total[..., None]).reshape(weighted.shape[0], D))


def block_back(query_heads, grad_heads, log_total, delta, piece_keys, piece_values, allowed):
    key_heads = split_heads(piece_keys)
    value_heads = split_heads(piece_values)
    scores = jnp.einsum("qhd,khd->qhk", query_heads, key_heads, preferred_element_type=jnp.float32)
    weights = jnp.exp(jnp.where(allowed[:, None, :], scores - log_total[..., None], NEGATIVE))
    grad_weights = jnp.einsum(
        "qhd,khd->qhk", grad_heads, value_heads, preferred_element_type=jnp.float32
    )
    grad_scores = (weights * (grad_weights - delta[..., None])).astype(jnp.bfloat16)
    grad_values = jnp.einsum(
        "qhk,qhd->khd", weights.astype(jnp.bfloat16), grad_heads, preferred_element_type=jnp.float32
    )
    grad_keys = jnp.einsum(
        "qhk,qhd->khd", grad_scores, query_heads, preferred_element_type=jnp.float32
    )
    grad_query = jnp.einsum(
        "qhk,khd->qhd", grad_scores, key_heads, preferred_element_type=jnp.float32
    )
    return (grad_query, grad_keys, grad_values)


def scan_back(
    query_heads,
    grad_heads,
    log_total,
    delta,
    all_keys,
    all_values,
    row_doc,
    row_pos,
    order,
    lengths,
    blocksize,
    causal,
):
    total_keys = all_keys.shape[0]
    width = math.gcd(total_keys, 512)
    count = total_keys // width

    def step(grad_query, item):
        block_keys, block_values, number = item
        key_doc, key_pos = locate(order, lengths, blocksize, number * width, width)
        allowed = visible(row_doc, row_pos, key_doc, key_pos, causal)
        query_term, key_term, value_term = block_back(
            query_heads, grad_heads, log_total, delta, block_keys, block_values, allowed
        )
        return (grad_query + query_term, (key_term, value_term))

    grad_query, (grad_keys, grad_values) = lax.scan(
        step,
        jnp.zeros(query_heads.shape, jnp.float32),
        (
            all_keys.reshape(count, width, D),
            all_values.reshape(count, width, D),
            jnp.arange(count, dtype=jnp.int32),
        ),
    )
    return (grad_query, grad_keys.reshape(total_keys, D), grad_values.reshape(total_keys, D))


def on_device(
    inputs,
    memory,
    target_lengths,
    source_lengths,
    target_order,
    source_order,
    self_gain,
    self_shift,
    self_query,
    query_bias,
    self_key,
    self_value,
    value_bias,
    self_output,
    output_bias,
    cross_gain,
    cross_shift,
    cross_query,
    cquery_bias,
    cross_key,
    cross_value,
    cvalue_bias,
    cross_output,
    coutput_bias,
    final_gain,
    final_shift,
    inner_weight,
    inner_bias,
    outer_weight,
    outer_bias,
    cotangent,
):
    rows = inputs.shape[1]
    sources = memory.shape[1]
    target_half = rows // 2
    source_half = sources // 2
    own_lengths = target_lengths[0]
    memory_lengths = source_lengths[0]
    own_order = target_order[0]
    memory_order = source_order[0]
    scale = float(D // HEADS) ** (-0.5)
    place = lax.axis_index("seq")
    row_doc, row_pos = locate(own_order, own_lengths, target_half, place * rows, rows)
    inputs_f = inputs[0].astype(jnp.float32)
    encoded = memory[0]
    normed, norm_back = jax.vjp(
        norm, inputs_f, self_gain.astype(jnp.float32), self_shift.astype(jnp.float32)
    )
    normed_low = normed.astype(jnp.bfloat16)
    queries = ((product(normed_low, self_query) + query_bias) * scale).astype(jnp.bfloat16)
    keys = product(normed_low, self_key).astype(jnp.bfloat16)
    values = (product(normed_low, self_value) + value_bias).astype(jnp.bfloat16)
    query_heads = split_heads(queries)
    piece = (
        lax.all_gather(keys, "seq", axis=0, tiled=True),
        lax.all_gather(values, "seq", axis=0, tiled=True),
    )
    key_doc, key_pos = locate(own_order, own_lengths, target_half, jnp.int32(0), piece[0].shape[0])
    self_carry = online(
        opening(rows),
        query_heads,
        piece[0],
        piece[1],
        visible(row_doc, row_pos, key_doc, key_pos, True),
    )
    self_total, mixed = finish(self_carry)
    mixed_low = mixed.astype(jnp.bfloat16)
    middle = inputs_f + product(mixed_low, self_output) + output_bias
    crossed, cross_back = jax.vjp(
        norm, middle, cross_gain.astype(jnp.float32), cross_shift.astype(jnp.float32)
    )
    crossed_low = crossed.astype(jnp.bfloat16)
    cqueries = ((product(crossed_low, cross_query) + cquery_bias) * scale).astype(jnp.bfloat16)
    ckeys = product(encoded, cross_key).astype(jnp.bfloat16)
    cvalues = (product(encoded, cross_value) + cvalue_bias).astype(jnp.bfloat16)
    cquery_heads = split_heads(cqueries)
    piece = (
        lax.all_gather(ckeys, "seq", axis=0, tiled=True),
        lax.all_gather(cvalues, "seq", axis=0, tiled=True),
    )
    key_doc, key_pos = locate(
        memory_order, memory_lengths, source_half, jnp.int32(0), piece[0].shape[0]
    )
    cross_carry = online(
        opening(rows),
        cquery_heads,
        piece[0],
        piece[1],
        visible(row_doc, row_pos, key_doc, key_pos, False),
    )
    cross_total, heard = finish(cross_carry)
    heard_low = heard.astype(jnp.bfloat16)
    later = middle + product(heard_low, cross_output) + coutput_bias
    fed, final_back = jax.vjp(
        norm, later, final_gain.astype(jnp.float32), final_shift.astype(jnp.float32)
    )
    fed_low = fed.astype(jnp.bfloat16)
    before = product(fed_low, inner_weight) + inner_bias
    after, gelu_back = jax.vjp(lambda entry: jax.nn.gelu(entry, approximate=False), before)
    after_low = after.astype(jnp.bfloat16)
    result = later + product(after_low, outer_weight) + outer_bias
    grad_out = cotangent[0]
    outer_weight_grad = weight_grad(after_low, grad_out)
    outer_bias_grad = jnp.sum(grad_out.astype(jnp.float32), axis=0)
    grad_after = input_grad(grad_out, outer_weight)
    grad_before = gelu_back(grad_after)[0].astype(jnp.bfloat16)
    inner_weight_grad = weight_grad(fed_low, grad_before)
    inner_bias_grad = jnp.sum(grad_before.astype(jnp.float32), axis=0)
    grad_fed = input_grad(grad_before, inner_weight)
    grad_later_norm, final_gain_grad, final_shift_grad = final_back(grad_fed)
    grad_later = cotangent[0].astype(jnp.float32) + grad_later_norm
    grad_cbranch = grad_later.astype(jnp.bfloat16)
    cross_output_grad = weight_grad(heard_low, grad_cbranch)
    coutput_bias_grad = jnp.sum(grad_cbranch.astype(jnp.float32), axis=0)
    grad_heard = input_grad(grad_cbranch, cross_output).astype(jnp.bfloat16)
    grad_heard_heads = split_heads(grad_heard)
    cross_delta = jnp.sum(grad_heard_heads.astype(jnp.float32) * split_heads(heard), axis=-1)
    all_ckeys, all_cvalues = (
        lax.all_gather(ckeys, "seq", axis=0, tiled=True),
        lax.all_gather(cvalues, "seq", axis=0, tiled=True),
    )
    grad_cq, part_ckeys, part_cvalues = scan_back(
        cquery_heads,
        grad_heard_heads,
        cross_total,
        cross_delta,
        all_ckeys,
        all_cvalues,
        row_doc,
        row_pos,
        memory_order,
        memory_lengths,
        source_half,
        False,
    )
    own_ckeys, own_cvalues = (
        lax.psum_scatter(
            part_ckeys.astype(jnp.bfloat16), "seq", scatter_dimension=0, tiled=True
        ).astype(jnp.float32),
        lax.psum_scatter(
            part_cvalues.astype(jnp.bfloat16), "seq", scatter_dimension=0, tiled=True
        ).astype(jnp.float32),
    )
    own_ckeys_low = own_ckeys.astype(jnp.bfloat16)
    own_cvalues_low = own_cvalues.astype(jnp.bfloat16)
    cross_key_grad = weight_grad(encoded, own_ckeys_low)
    cross_value_grad = weight_grad(encoded, own_cvalues_low)
    cvalue_bias_grad = jnp.sum(own_cvalues_low.astype(jnp.float32), axis=0)
    memory_grad = input_grad(own_ckeys_low, cross_key) + input_grad(own_cvalues_low, cross_value)
    grad_cq_low = grad_cq.reshape(rows, D).astype(jnp.bfloat16)
    cross_query_grad = weight_grad(crossed_low, grad_cq_low) * scale
    cquery_bias_grad = jnp.sum(grad_cq_low.astype(jnp.float32), axis=0) * scale
    grad_crossed = input_grad(grad_cq_low, cross_query) * scale
    grad_middle_norm, cross_gain_grad, cross_shift_grad = cross_back(grad_crossed)
    grad_middle = grad_later + grad_middle_norm
    grad_sbranch = grad_middle.astype(jnp.bfloat16)
    self_output_grad = weight_grad(mixed_low, grad_sbranch)
    output_bias_grad = jnp.sum(grad_sbranch.astype(jnp.float32), axis=0)
    grad_mixed = input_grad(grad_sbranch, self_output).astype(jnp.bfloat16)
    grad_mixed_heads = split_heads(grad_mixed)
    self_delta = jnp.sum(grad_mixed_heads.astype(jnp.float32) * split_heads(mixed), axis=-1)
    all_keys, all_values = (
        lax.all_gather(keys, "seq", axis=0, tiled=True),
        lax.all_gather(values, "seq", axis=0, tiled=True),
    )
    grad_q, part_keys, part_values = scan_back(
        query_heads,
        grad_mixed_heads,
        self_total,
        self_delta,
        all_keys,
        all_values,
        row_doc,
        row_pos,
        own_order,
        own_lengths,
        target_half,
        True,
    )
    own_keys, own_values = (
        lax.psum_scatter(
            part_keys.astype(jnp.bfloat16), "seq", scatter_dimension=0, tiled=True
        ).astype(jnp.float32),
        lax.psum_scatter(
            part_values.astype(jnp.bfloat16), "seq", scatter_dimension=0, tiled=True
        ).astype(jnp.float32),
    )
    own_keys_low = own_keys.astype(jnp.bfloat16)
    own_values_low = own_values.astype(jnp.bfloat16)
    self_key_grad = weight_grad(normed_low, own_keys_low)
    self_value_grad = weight_grad(normed_low, own_values_low)
    value_bias_grad = jnp.sum(own_values_low.astype(jnp.float32), axis=0)
    grad_q_low = grad_q.reshape(rows, D).astype(jnp.bfloat16)
    self_query_grad = weight_grad(normed_low, grad_q_low) * scale
    query_bias_grad = jnp.sum(grad_q_low.astype(jnp.float32), axis=0) * scale
    grad_normed = (
        input_grad(grad_q_low, self_query) * scale
        + input_grad(own_keys_low, self_key)
        + input_grad(own_values_low, self_value)
    )
    grad_in_norm, self_gain_grad, self_shift_grad = norm_back(grad_normed)
    inputs_grad = grad_middle + grad_in_norm
    summed = lax.psum(
        (
            self_gain_grad,
            self_shift_grad,
            self_query_grad,
            query_bias_grad,
            self_key_grad,
            self_value_grad,
            value_bias_grad,
            self_output_grad,
            output_bias_grad,
            cross_gain_grad,
            cross_shift_grad,
            cross_query_grad,
            cquery_bias_grad,
            cross_key_grad,
            cross_value_grad,
            cvalue_bias_grad,
            cross_output_grad,
            coutput_bias_grad,
            final_gain_grad,
            final_shift_grad,
            inner_weight_grad,
            inner_bias_grad,
            outer_weight_grad,
            outer_bias_grad,
        ),
        ("seq", "batch"),
    )
    return (result.astype(jnp.bfloat16)[None], inputs_grad[None], memory_grad[None]) + tuple(summed)


def solution(mesh):
    in_specs = (
        P("batch", "seq", None),
        P("batch", "seq", None),
        P("batch", None),
        P("batch", None),
        P("batch", None),
        P("batch", None),
        P(),
        P(),
        P(),
        P(),
        P(),
        P(),
        P(),
        P(),
        P(),
        P(),
        P(),
        P(),
        P(),
        P(),
        P(),
        P(),
        P(),
        P(),
        P(),
        P(),
        P(),
        P(),
        P(),
        P(),
        P("batch", "seq", None),
    )
    out_specs = (
        P("batch", "seq", None),
        P("batch", "seq", None),
        P("batch", "seq", None),
        P(),
        P(),
        P(),
        P(),
        P(),
        P(),
        P(),
        P(),
        P(),
        P(),
        P(),
        P(),
        P(),
        P(),
        P(),
        P(),
        P(),
        P(),
        P(),
        P(),
        P(),
        P(),
        P(),
        P(),
    )
    return jax.shard_map(
        on_device, mesh=mesh, in_specs=in_specs, out_specs=out_specs, check_vma=False
    )
```

profile of v0, /device:TPU:0, one launch (start us, length us, event | category | flops | bytes accessed | tf_op | source)
XLA Modules:
  0.0 903.0 jit_solution(3059865361738786845)
XLA Ops:
  41.5 25.6 %all-gather.9.cloned.1.call-done = bf16[1536,512]{1,0:T(8,128)(2,1)} async-done(((bf16[192,512]{1,0:T(8,128)(2,1)}), bf16[1536,512]{1,0:T(8,128)(2,1)}) %all-gather.9.cloned.1.call-update) | async-done | bytes 1572880 | tf_op jit(solution)/shard_map/all_gather | solution.py:230
  69.7 32.2 %all-gather.7.cloned.1.call-done = bf16[3072,512]{1,0:T(8,128)(2,1)} async-done(((bf16[384,512]{1,0:T(8,128)(2,1)}), bf16[3072,512]{1,0:T(8,128)(2,1)}) %all-gather.7.cloned.1.call-update) | async-done | bytes 3145744 | tf_op jit(solution)/shard_map/all_gather | solution.py:206
  102.0 4.6 copy.148
  106.6 16.6 %fusion.50 = (f32[384,8]{0,1:T(8,128)S(1)}, f32[8,3072,384]{2,1,0:T(8,128)}) fusion(pred[384,3072]{0,1:T(8,128)(4,1)} %compare_and_fusion.1, bf16[3072,8,64]{0,2,1:T(8,128)(2,1)} %bitcast.395, bf16[384,8,64]{0,2,1:T(8,128)(2,1)S(1)} %bitcast.391), kind=kOutput, calls=%fused_computation.70 | convolution fusion | flops 1226830848 | bytes 42479616 | tf_op jit(solution)/shard_map/qhd,khd->qhk/dot_general | solution.py:70
  123.8 16.1 %fusion.53 = f32[384,8]{0,1:T(8,128)S(1)} fusion(f32[8,3072,384]{2,1,0:T(8,128)} %get-tuple-element.834, f32[384,8]{0,1:T(8,128)S(1)} %broadcast_maximum_fusion.1, pred[384,3072]{0,1:T(8,128)(4,1)S(1)} %copy-done.11), kind=kLoop, calls=%fused_computation.73 | loop fusion | flops 28308480 | bytes 38952960 | tf_op jit(solution)/shard_map/reduce_sum | solution.py:76
  139.9 4.7 copy.146
  144.6 18.2 %fusion.173 = (bf16[384,8,64]{0,2,1:T(8,128)(2,1)}, f32[384,8,64]{0,2,1:T(8,128)}) fusion(f32[384,8]{0,1:T(8,128)S(1)} %fusion.53, bf16[3072,8,64]{0,2,1:T(8,128)(2,1)} %bitcast.403, f32[8,3072,384]{2,1,0:T(8,128)} %get-tuple-element.834, f32[384,8]{0,1:T(8,128)S(1)} %broadcast_maximum_fusion.1, pred[384,3072]{0,1:T(8,128)(4,1)S(1)} %copy-done.12), kind=kOutput, calls=%fused_computation.276 | convolution fusion | flops 1236664320 | bytes 43278336 | tf_op jit(solution)/shard_map/qhk,khd->qhd/dot_general | solution.py:77
  168.4 10.8 %fusion.55 = (f32[384,8]{0,1:T(8,128)S(1)}, f32[8,1536,384]{2,1,0:T(8,128)}) fusion(pred[384,1536]{0,1:T(8,128)(4,1)} %broadcast_compare_fusion.1, bf16[1536,8,64]{0,2,1:T(8,128)(2,1)} %bitcast.402, bf16[384,8,64]{0,2,1:T(8,128)(2,1)S(1)} %bitcast.393), kind=kOutput, calls=%fused_computation.77 | convolution fusion | flops 613413888 | bytes 21442560 | tf_op jit(solution)/shard_map/qhd,khd->qhk/dot_general | solution.py:70
  179.2 9.7 %fusion.61 = f32[384,8]{0,1:T(8,128)S(1)} fusion(f32[8,1536,384]{2,1,0:T(8,128)} %get-tuple-element.840, f32[384,8]{0,1:T(8,128)S(1)} %broadcast_maximum_fusion, pred[384,1536]{0,1:T(8,128)(4,1)} %broadcast_compare_fusion.1), kind=kLoop, calls=%fused_computation.82 | loop fusion | flops 14152704 | bytes 19488768 | tf_op jit(solution)/shard_map/reduce_sum | solution.py:76
  189.5 12.1 %fusion.175 = (bf16[384,8,64]{0,2,1:T(8,128)(2,1)S(1)}, f32[384,8,64]{0,2,1:T(8,128)}) fusion(f32[384,8]{0,1:T(8,128)S(1)} %fusion.61, bf16[1536,8,64]{0,2,1:T(8,128)(2,1)} %bitcast.406, f32[8,1536,384]{2,1,0:T(8,128)} %get-tuple-element.840, f32[384,8]{0,1:T(8,128)S(1)} %broadcast_maximum_fusion, pred[384,1536]{0,1:T(8,128)(4,1)} %broadcast_compare_fusion.1), kind=kOutput, calls=%fused_computation.278 | convolution fusion | flops 618528768 | bytes 22241280 | tf_op jit(solution)/shard_map/qhk,khd->qhd/dot_general | solution.py:77
  202.4 9.1 %multiply_convert_fusion = (bf16[384,2048]{1,0:T(8,128)(2,1)}, f32[384,2048]{1,0:T(8,128)S(1)}, f32[384,2048]{1,0:T(8,128)S(1)}) fusion(f32[2048]{0:T(1024)S(1)} %copy-done.94, bf16[512,2048]{1,0:T(8,128)(2,1)S(1)} %copy-done, f32[384,512]{1,0:T(8,128)S(1)} %get-tuple-element.844, f32[512]{0:T(512)S(1)} %convert_element_type.275, ...), kind=kOutput, calls=%fused_computation.91 | convolution fusion | flops 858193920 | bytes 10763264 | tf_op jit(solution)/shard_map/dot_general | solution.py:23
  219.2 70.5 %while.34 = (s32[]{:T(128)}, f32[384,8,64]{0,2,1:T(8,128)}, bf16[3,512,8,64]{1,3,2,0:T(8,128)(2,1)}, bf16[3,512,8,64]{1,3,2,0:T(8,128)(2,1)}, bf16[3,512,512]{2,...) while((s32[]{:T(128)}, f32[384,8,64]{0,2,1:T(8,128)}, ...), condition=%wide.region_25.26_spmd.clone, body=%wide.region_22.25_spmd.clone.sunk | while | flops 1019889152 | bytes 46046948 | solution.py:139
  223.3 3.7 fusion.289
  228.0 4.9 fusion.291
  237.5 5.2 fusion.294
  246.6 3.7 fusion.289
  251.3 4.9 fusion.291
  261.0 5.2 fusion.294
  270.2 3.7 fusion.289
  274.8 4.9 fusion.291
  284.6 5.2 fusion.294
  289.8 4.9 copy.187
  294.7 5.5 reshape.662
  305.8 3.7 copy.186
  315.8 148.5 %while.35 = (s32[]{:T(128)}, f32[384,8,64]{0,2,1:T(8,128)}, bf16[6,512,8,64]{1,3,2,0:T(8,128)(2,1)}, bf16[6,512,8,64]{1,3,2,0:T(8,128)(2,1)}, bf16[6,512,512]{2,...) while((s32[]{:T(128)}, f32[384,8,64]{0,2,1:T(8,128)}, ...), condition=%wide.region_33.34_spmd.clone, body=%wide.region_30.33_spmd.clone.sunk | while | flops 1020282368 | bytes 44477180 | solution.py:139
  325.8 5.0 fusion.307
  335.4 5.1 fusion.310
  345.7 3.7 fusion.305
  350.3 5.2 fusion.307
  360.4 5.3 fusion.310
  370.8 3.7 fusion.305
  375.5 4.9 fusion.307
  385.2 5.1 fusion.310
  400.1 4.9 fusion.307
  409.9 5.1 fusion.310
  424.8 4.9 fusion.307
  434.5 5.1 fusion.310
  444.7 3.7 fusion.305
  449.4 4.9 fusion.307
  459.2 5.1 fusion.310
  464.3 7.8 copy.185
  472.1 9.3 %reshape.658 = bf16[3072,512]{1,0:T(8,128)(2,1)} reshape(bf16[6,512,8,64]{3,2,1,0:T(8,128)(2,1)} %copy.185) | data formatting | bytes 6291456
  481.5 7.9 copy.184
  489.5 9.5 %reshape.656 = bf16[3072,512]{1,0:T(8,128)(2,1)} reshape(bf16[6,512,8,64]{3,2,1,0:T(8,128)(2,1)} %copy.184) | data formatting | bytes 6291456
  519.5 8.5 reduce-scatter.15.cloned.1.call-done
  530.6 47.4 %reduce-scatter.13.cloned.1.call-done = bf16[384,512]{1,0:T(8,128)(2,1)} async-done(((bf16[3072,512]{1,0:T(8,128)(2,1)}), bf16[384,512]{1,0:T(8,128)(2,1)}) %reduce-scatter.13.cloned.1.call-update) | async-done | bytes 393232
  600.0 42.4 %all-reduce = (f32[512]{0:T(512)}, f32[512]{0:T(512)}, f32[512]{0:T(512)}, f32[512]{0:T(512)}, f32[512]{0:T(512)}, /*index=5*/f32[512]{0:T(512)}, f32[512]{0:T(5...) all-reduce(f32[512]{0:T(512)S(1)} %get-tuple-element.726, ...), channel_id=1, replica_groups=mesh['seq'=8,'batch'=4] {'seq','batch'}, use_global_device_ids=true, to_apply=%region_41.42 | all-reduce | flops 8704 | bytes 69632 | tf_op jit(solution)/shard_map/psum | solution.py:354
  643.6 235.3 %all-reduce.4.cloned.1.call-done = (f32[512,512]{1,0:T(8,128)}, f32[512,512]{1,0:T(8,128)}, f32[512,512]{1,0:T(8,128)}, f32[512,512]{1,0:T(8,128)}, f32[512,512]...) async-done(((f32[512,512]{1,0:T(8,128)}, f32[512,512]{1,0:T(8,128)}, ...) | async-done | bytes 16777232 | tf_op jit(solution)/shard_map/psum | solution.py:354
  (589 shorter events, 224.8 us)
Async XLA Ops:
  7.2 195.2 %copy-start = (bf16[512,2048]{1,0:T(8,128)(2,1)S(1)}, bf16[512,2048]{1,0:T(8,128)(2,1)}, u32[]{:S(2)}) copy-start(bf16[512,2048]{1,0:T(8,128)(2,1)} %param.61) | copy-start | bytes 6291460
  7.2 12.7 %copy-start.13 = (bf16[1,384,512]{2,1,0:T(8,128)(2,1)S(1)}, bf16[1,384,512]{2,1,0:T(8,128)(2,1)}, u32[]{:S(2)}) copy-start(bf16[1,384,512]{2,1,0:T(8,128)(2,1)} %param.35) | copy-start | bytes 1179652
  7.2 12.7 %copy-start.55 = (bf16[512,512]{1,0:T(8,128)(2,1)S(1)}, bf16[512,512]{1,0:T(8,128)(2,1)}, u32[]{:S(2)}) copy-start(bf16[512,512]{1,0:T(8,128)(2,1)} %param.46) | copy-start | bytes 1572868
  7.2 31.7 %all-gather.11.cloned.1.call-start = ((), (), s32[]{:S(2)}) async-start(), calls=%async_computation.7 | async-start | bytes 1769472 | tf_op jit(solution)/shard_map/all_gather | solution.py:229
  9.5 57.6 %all-gather.9.cloned.1.call-start = ((), (), s32[]{:S(2)}) async-start(), calls=%async_computation.6 | async-start | bytes 1769472 | tf_op jit(solution)/shard_map/all_gather | solution.py:230
  12.4 10.3 %copy-start.73 = (s32[1,16]{1,0:T(1,128)S(1)}, s32[1,16]{1,0:T(1,128)}, u32[]{:S(2)}) copy-start(s32[1,16]{1,0:T(1,128)} %param.39) | copy-start | bytes 196
  12.4 13.2 %copy-start.54 = (bf16[512,512]{1,0:T(8,128)(2,1)S(1)}, bf16[512,512]{1,0:T(8,128)(2,1)}, u32[]{:S(2)}) copy-start(bf16[512,512]{1,0:T(8,128)(2,1)} %param.43) | copy-start | bytes 1572868
  12.4 89.6 %all-gather.7.cloned.1.call-start = ((), (), s32[]{:S(2)}) async-start(), calls=%async_computation.5 | async-start | bytes 3538944 | tf_op jit(solution)/shard_map/all_gather | solution.py:206
  13.2 13.5 %copy-start.65 = (f32[512]{0:T(512)}, f32[512]{0:T(512)S(1)}, u32[]{:S(2)}) copy-start(f32[512]{0:T(512)S(1)} %convert_element_type.247) | copy-start | bytes 6148
  15.0 10.5 %copy-start.62 = (f32[384]{0:T(512)}, f32[384]{0:T(512)S(1)}, u32[]{:S(2)}) copy-start(f32[384]{0:T(512)S(1)} %broadcast_multiply_fusion.5) | copy-start | bytes 4612
  16.8 9.9 %copy-start.74 = (f32[384]{0:T(512)}, f32[384]{0:T(512)S(1)}, u32[]{:S(2)}) copy-start(f32[384]{0:T(512)S(1)} %fusion.151) | copy-start | bytes 4612
  19.2 120.7 %all-gather.5.cloned.1.call-start = ((), (), s32[]{:S(2)}) async-start(), calls=%async_computation.4 | async-start | bytes 3538944 | tf_op jit(solution)/shard_map/all_gather | solution.py:207
  21.8 9.3 %copy-start.110 = (bf16[512]{0:T(512)(128)(2,1)S(1)}, bf16[512]{0:T(512)(128)(2,1)}, u32[]{:S(2)}) copy-start(bf16[512]{0:T(512)(128)(2,1)} %param.49) | copy-start | bytes 3076
  21.8 9.3 %copy-start.102 = (bf16[512]{0:T(512)(128)(2,1)S(1)}, bf16[512]{0:T(512)(128)(2,1)}, u32[]{:S(2)}) copy-start(bf16[512]{0:T(512)(128)(2,1)} %param.50) | copy-start | bytes 3076
  21.8 9.3 %copy-start.111 = (bf16[512]{0:T(512)(128)(2,1)S(1)}, bf16[512]{0:T(512)(128)(2,1)}, u32[]{:S(2)}) copy-start(bf16[512]{0:T(512)(128)(2,1)} %param.51) | copy-start | bytes 3076
  21.8 9.3 %copy-start.112 = (bf16[512]{0:T(512)(128)(2,1)S(1)}, bf16[512]{0:T(512)(128)(2,1)}, u32[]{:S(2)}) copy-start(bf16[512]{0:T(512)(128)(2,1)} %param.53) | copy-start | bytes 3076
  21.8 9.4 %copy-start.113 = (bf16[512]{0:T(512)(128)(2,1)S(1)}, bf16[512]{0:T(512)(128)(2,1)}, u32[]{:S(2)}) copy-start(bf16[512]{0:T(512)(128)(2,1)} %param.58) | copy-start | bytes 3076
  21.9 9.4 %copy-start.114 = (bf16[512]{0:T(512)(128)(2,1)S(1)}, bf16[512]{0:T(512)(128)(2,1)}, u32[]{:S(2)}) copy-start(bf16[512]{0:T(512)(128)(2,1)} %param.59) | copy-start | bytes 3076
  21.9 9.4 %copy-start.115 = (bf16[512]{0:T(512)(128)(2,1)S(1)}, bf16[512]{0:T(512)(128)(2,1)}, u32[]{:S(2)}) copy-start(bf16[512]{0:T(512)(128)(2,1)} %param.60) | copy-start | bytes 3076
  21.9 9.4 %copy-start.101 = (bf16[2048]{0:T(1024)(128)(2,1)S(1)}, bf16[2048]{0:T(1024)(128)(2,1)}, u32[]{:S(2)}) copy-start(bf16[2048]{0:T(1024)(128)(2,1)} %param.62) | copy-start | bytes 12292
  21.9 492.8 %reduce-scatter.19.cloned.1.call-start = ((), (), s32[]{:S(2)}) async-start(), calls=%async_computation.11 | async-start | bytes 1769472
  22.8 18.7 %copy-start.57 = (s32[384]{0:T(512)}, s32[384]{0:T(512)S(1)}, u32[]{:S(2)}) copy-start(s32[384]{0:T(512)S(1)} %fusion.145) | copy-start | bytes 4612
  31.1 75.5 %copy-start.4 = (bf16[384,512]{0,1:T(8,128)(2,1)}, bf16[384,512]{0,1:T(8,128)(2,1)S(1)}, u32[]{:S(2)}) copy-start(bf16[384,512]{0,1:T(8,128)(2,1)S(1)} %copy.149) | copy-start | bytes 1179652
  31.2 133.7 %copy-start.97 = (f32[512]{0:T(512)}, f32[512]{0:T(512)S(1)}, u32[]{:S(2)}) copy-start(f32[512]{0:T(512)S(1)} %convert_element_type.265) | copy-start | bytes 6148
  31.2 133.7 %copy-start.99 = (f32[512]{0:T(512)}, f32[512]{0:T(512)S(1)}, u32[]{:S(2)}) copy-start(f32[512]{0:T(512)S(1)} %convert_element_type.266) | copy-start | bytes 6148
  31.3 171.1 %copy-start.60 = (f32[512]{0:T(512)}, f32[512]{0:T(512)S(1)}, u32[]{:S(2)}) copy-start(f32[512]{0:T(512)S(1)} %convert_element_type.275) | copy-start | bytes 6148
  106.6 17.2 %copy-start.11 = (pred[384,3072]{0,1:T(8,128)(4,1)S(1)}, pred[384,3072]{0,1:T(8,128)(4,1)}, u32[]{:S(2)}) copy-start(pred[384,3072]{0,1:T(8,128)(4,1)} %compare_and_fusion.1) | copy-start | bytes 3538948
  164.6 37.0 %copy-start.8 = (f32[384,512]{1,0:T(8,128)}, f32[384,512]{1,0:T(8,128)S(1)}, u32[]{:S(2)}) copy-start(f32[384,512]{1,0:T(8,128)S(1)} %get-tuple-element.838) | copy-start | bytes 2359300
  189.5 12.1 %copy-start.32 = (bf16[512,512]{1,0:T(8,128)(2,1)S(1)}, bf16[512,512]{1,0:T(8,128)(2,1)}, u32[]{:S(2)}) copy-start(bf16[512,512]{1,0:T(8,128)(2,1)} %param.57) | copy-start | bytes 1572868
  201.6 10.0 %copy-start.34 = (bf16[384,8,64]{0,2,1:T(8,128)(2,1)}, bf16[384,8,64]{0,2,1:T(8,128)(2,1)S(1)}, u32[]{:S(2)}) copy-start(bf16[384,8,64]{0,2,1:T(8,128)(2,1)S(1)} %get-tuple-element.841) | copy-start | bytes 1179652
  202.1 13.7 %copy-start.15 = (f32[384,512]{1,0:T(8,128)}, f32[384,512]{1,0:T(8,128)S(1)}, u32[]{:S(2)}) copy-start(f32[384,512]{1,0:T(8,128)S(1)} %get-tuple-element.844) | copy-start | bytes 2359300
  202.4 13.4 %copy-start.68 = (f32[384]{0:T(512)}, f32[384]{0:T(512)S(1)}, u32[]{:S(2)}) copy-start(f32[384]{0:T(512)S(1)} %fusion.153) | copy-start | bytes 4612
  202.4 9.2 %copy-start.25 = (bf16[1,384,512]{2,1,0:T(8,128)(2,1)S(1)}, bf16[1,384,512]{2,1,0:T(8,128)(2,1)}, u32[]{:S(2)}) copy-start(bf16[1,384,512]{2,1,0:T(8,128)(2,1)} %param.65) | copy-start | bytes 1179652
  202.4 9.2 %copy-start.116 = (bf16[2048,512]{1,0:T(8,128)(2,1)S(1)}, bf16[2048,512]{1,0:T(8,128)(2,1)}, u32[]{:S(2)}) copy-start(bf16[2048,512]{1,0:T(8,128)(2,1)} %param.63) | copy-start | bytes 6291460
  294.7 6.5 copy-start.9
  294.7 6.5 copy-start.71
  294.7 6.5 copy-start.84
  294.7 6.5 copy-start.117
  300.3 216.9 %reduce-scatter.17.cloned.1.call-start = ((), (), s32[]{:S(2)}) async-start(), calls=%async_computation.10 | async-start | bytes 1769472
  309.5 6.3 copy-start.5
  309.5 6.3 copy-start.58
  315.7 212.3 %reduce-scatter.15.cloned.1.call-start = ((), (), s32[]{:S(2)}) async-start(), calls=%async_computation.9 | async-start | bytes 3538944
  481.5 96.6 %reduce-scatter.13.cloned.1.call-start = ((), (), s32[]{:S(2)}) async-start(), calls=%async_computation.8 | async-start | bytes 3538944
  499.1 379.9 %all-reduce.4.cloned.1.call-start = ((), (), s32[]{:S(2)}) async-start(), calls=%async_computation.12 | async-start | bytes 33554432 | tf_op jit(solution)/shard_map/psum | solution.py:354
  500.9 7.1 copy-start.45
  514.8 63.3 %copy-start.67 = (f32[512]{0:T(512)S(1)}, f32[512]{0:T(512)}, u32[]{:S(2)}) copy-start(f32[512]{0:T(512)} %copy-done.65) | copy-start | bytes 6148
  514.8 63.3 %copy-start.75 = (f32[384]{0:T(512)S(1)}, f32[384]{0:T(512)}, u32[]{:S(2)}) copy-start(f32[384]{0:T(512)} %copy-done.74) | copy-start | bytes 4612
  514.8 63.3 %copy-start.109 = (f32[512]{0:T(512)S(1)}, f32[512]{0:T(512)}, u32[]{:S(2)}) copy-start(f32[512]{0:T(512)} %copy-done.108) | copy-start | bytes 6148
  (129 other events, 460.4 us)
Sparse Core Ops, SparseCore 0:
  10.5 28.3 all-gather.10
  41.4 25.6 all-gather.8
  69.6 32.3 all-gather.6
  104.3 32.3 all-gather.4
  300.4 38.6 reduce-scatter.18
  342.2 38.4 reduce-scatter.16
  481.6 46.3 reduce-scatter.14
  531.8 46.2 reduce-scatter.12
  586.8 292.1 all-reduce.3
where the time goes:
time: 915 us; the launch traced here: 903 us
  waiting for transfers between devices  353 us (39%)
  matrix products  289 us (32%)
  local copies, waits for them, and re-layouts  123 us (13%)
  other arithmetic  72.6 us (8%)
  blocking collectives  42.4 us (5%)
  between operations  15.6 us (2%)
    psum x1, waiting for transfers between devices, on_device(): lax.psum((self_gain_grad, self_shift_grad, self_query_grad, query_bias_gr...  235 us
    unnamed x236, local copies, waits for them, and re-layouts  74.2 us
    unnamed x13, waiting for transfers between devices  56.1 us
    dot_general x9, matrix products, block_back(): jnp.einsum('qhk,qhd->khd', weights.astype(jnp.bfloat16), grad_heads, pref...  46.4 us
    dot_general x9, matrix products, block_back(): jnp.einsum('qhd,khd->qhk', grad_heads, value_heads, preferred_element_typ...  44.9 us
    psum x1, blocking collectives, on_device(): lax.psum((self_gain_grad, self_shift_grad, self_query_grad, query_bias_gr...  42.4 us
    dot_general x9, matrix products, block_back(): jnp.einsum('qhd,khd->qhk', query_heads, key_heads, preferred_element_type...  33.1 us
    all_gather x1, waiting for transfers between devices, on_device(): lax.all_gather(keys, 'seq', axis=0, tiled=True)  32.2 us
  transfers between devices with their start and end apart: 9, of which 6 were waited for; matrix products, arithmetic and copies ran while one was open for 33% of the time, Pallas kernels for 0%

commit v1 on v0

--- a/solution.py
+++ b/solution.py
@@ -3,6 +3,8 @@
 import jax
 import jax.numpy as jnp
 from jax import lax
+from jax.experimental import pallas as pl
+from jax.experimental.pallas import tpu as pltpu
 from jax.sharding import PartitionSpec as P
 
 D = 512
@@ -383,6 +385,1192 @@
     return (result.astype(jnp.bfloat16)[None], inputs_grad[None], memory_grad[None]) + tuple(summed)
 
 
+HDIM = D // HEADS
+SHORTEST = 32
+LONGEST = 1024
+CHUNK = 256
+PIECE = 64
+MESH = pl.DeviceIdType.MESH
+PARTS = 2
+BF = jnp.bfloat16
+F32 = jnp.float32
+VECTORS = 24
+
+
+def nn(left, right):
+    return lax.dot_general(left, right, (((1,), (0,)), ((), ())), preferred_element_type=F32)
+
+
+def nt(left, right):
+    return lax.dot_general(left, right, (((1,), (1,)), ((), ())), preferred_element_type=F32)
+
+
+def tn(left, right):
+    return lax.dot_general(left, right, (((0,), (0,)), ((), ())), preferred_element_type=F32)
+
+
+def centred(values):
+    center = values - jnp.mean(values, axis=-1, keepdims=True)
+    spread = lax.rsqrt(jnp.mean(center * center, axis=-1, keepdims=True) + EPSILON)
+    return center * spread, spread
+
+
+def norm_back(grad, unit, spread, gain):
+    scaled = grad * gain
+    return spread * (
+        scaled
+        - jnp.mean(scaled, axis=-1, keepdims=True)
+        - unit * jnp.mean(scaled * unit, axis=-1, keepdims=True)
+    )
+
+
+def column_sum(values):
+    return jnp.sum(values, axis=0, keepdims=True)
+
+
+def spread_heads(block, heads):
+    lane = lax.broadcasted_iota(jnp.int32, block.shape, 1)
+    return jnp.concatenate(
+        [
+            jnp.where((lane >= h * HDIM) & (lane < (h + 1) * HDIM), block, 0.0)
+            for h in range(heads)
+        ],
+        axis=0,
+    )
+
+
+def join_heads(stacked, heads):
+    rows = stacked.shape[0] // heads
+    lane = lax.broadcasted_iota(jnp.int32, (rows, stacked.shape[1]), 1)
+    total = stacked[:rows]
+    for h in range(1, heads):
+        total = jnp.where(lane >= h * HDIM, stacked[h * rows : (h + 1) * rows], total)
+    return total
+
+
+def part_of(array, index, size):
+    if len(array.shape) == 3:
+        count = size // PIECE
+        return array[pl.ds(index * count, count)].reshape(size, array.shape[2])
+    return array[pl.ds(pl.multiple_of(index * size, size), size), :]
+
+
+def whole_of(array):
+    return array[...].reshape(-1, array.shape[-1])
+
+
+def attend(queries, keys, values, low, high, scores, powers):
+    total = math.prod(keys.shape[:-1])
+    width = queries.shape[0]
+    chunk = total // PARTS
+    pieces = chunk // PIECE
+
+    def first(c, highest):
+        rows = pl.ds(pl.multiple_of(c * chunk, chunk), chunk)
+        place = lax.broadcasted_iota(jnp.int32, (chunk, width), 0) + c * chunk
+        found = jnp.where((place >= low) & (place < high), nt(part_of(keys, c, chunk), queries), NEGATIVE)
+        scores[rows, :] = found
+        return jnp.maximum(highest, jnp.max(found, axis=0, keepdims=True))
+
+    highest = lax.fori_loop(0, total // chunk, first, jnp.full((1, width), NEGATIVE, F32))
+
+    def second(c, summed):
+        rows = pl.ds(pl.multiple_of(c * chunk, chunk), chunk)
+        power = jnp.exp(scores[rows, :] - highest)
+        powers[pl.ds(c * pieces, pieces)] = power.astype(BF).reshape(pieces, PIECE, width)
+        return summed + column_sum(power)
+
+    summed = lax.fori_loop(0, total // chunk, second, jnp.zeros((1, width), F32))
+    inverse = 1.0 / summed
+    mixed = tn(whole_of(values), powers[0 : total // PIECE].reshape(total, width)) * inverse
+    return mixed.T, inverse
+
+
+def attend_back(queries, grads, product_of, keys, values, inverse, powers, store):
+    total = math.prod(keys.shape[:-1])
+    width = queries.shape[0]
+    chunk = total // PARTS
+    pieces = chunk // PIECE
+    ones = jnp.ones((8, queries.shape[1]), BF)
+    coarse = product_of.astype(BF)
+    fine = (product_of - coarse.astype(F32)).astype(BF)
+    delta = (nt(ones, coarse) + nt(ones, fine))[0:1]
+
+    def step(c, carry):
+        part = pl.ds(c * pieces, pieces)
+        weights = powers[part].reshape(chunk, width).astype(F32) * inverse
+        weights_low = weights.astype(BF)
+        change = (weights * (nt(part_of(values, c, chunk), grads) - delta)).astype(BF)
+        powers[part] = change.reshape(pieces, PIECE, width)
+        store(c, nn(change, queries), nn(weights_low, grads))
+        return carry
+
+    lax.fori_loop(0, total // chunk, step, 0)
+    return tn(whole_of(keys), powers[0 : total // PIECE].reshape(total, width)).T
+
+
+class Cube:
+    def __init__(self, me, level, levels):
+        self.me, self.level, self.levels = me, level, levels
+        self.bits = (lax.rem(me, 2), lax.rem(lax.div(me, 2), 2), lax.div(me, 4))
+
+    def other(self, code):
+        place = self.me
+        for axis in range(3):
+            if code >> axis & 1:
+                place = place + (1 << axis) * (1 - 2 * self.bits[axis])
+        return place
+
+    def plane(self, step):
+        return lax.rem(self.level + step, self.levels)
+
+    def greet(self):
+        barrier = pltpu.get_barrier_semaphore()
+        for code in (1, 2, 4):
+            pl.semaphore_signal(
+                barrier, inc=1, device_id={"seq": self.other(code)}, device_id_type=MESH
+            )
+        for step in range(1, self.levels):
+            pl.semaphore_signal(
+                barrier, inc=1, device_id={"batch": self.plane(step)}, device_id_type=MESH
+            )
+        pl.semaphore_wait(barrier, 2 + self.levels)
+
+    def send(self, code, source, target, send_sem, recv_sem):
+        copy = pltpu.make_async_remote_copy(
+            src_ref=source,
+            dst_ref=target,
+            send_sem=send_sem,
+            recv_sem=recv_sem,
+            device_id={"seq": self.other(code)},
+            device_id_type=MESH,
+        )
+        copy.start()
+        return copy
+
+
+class Steps:
+    def copies(self, step):
+        return [
+            pltpu.make_async_remote_copy(
+                src_ref=source,
+                dst_ref=target,
+                send_sem=self.send_sem.at[index],
+                recv_sem=self.recv_sem.at[index],
+                device_id=device,
+                device_id_type=MESH,
+            )
+            for device, source, target, index in self.moves(step)
+        ]
+
+    def begin(self, step):
+        for copy in self.copies(step):
+            copy.start()
+
+    def end(self, step):
+        for copy in self.copies(step):
+            copy.wait()
+
+    def advance(self, step):
+        self.end(step)
+        self.take(step)
+        self.begin(step + 1)
+
+
+class Reduce(Steps):
+    def __init__(self, cube, panels, first, pair, flat, edge, deep, leave, send_sem, recv_sem, sent):
+        self.cube, self.panels, self.first = cube, panels, first
+        self.pair, self.flat, self.edge, self.deep, self.leave = pair, flat, edge, deep, leave
+        self.send_sem, self.recv_sem, self.sent = send_sem, recv_sem, sent
+
+    def begin(self, step):
+        for index in {6: (1, 2), 8: (0,)}.get(step, ()):
+            pl.semaphore_wait(self.sent.at[index], 1)
+        if step == 4:
+            for k in range(1, self.cube.levels):
+                there = self.first + self.cube.plane(k)
+                for axis in (1, 2):
+                    self.leave[k - 1, axis - 1] = self.panels[there, self.rows(axis=axis, further=0), :]
+        super().begin(step)
+
+    def end(self, step):
+        super().end(step)
+        for index in {1: (0,), 3: (1, 2)}.get(step, ()):
+            pl.semaphore_signal(
+                self.sent.at[index],
+                inc=1,
+                device_id={"seq": self.cube.other(1 << index)},
+                device_id_type=MESH,
+            )
+
+    def rows(self, core=0, axis=None, far=0, further=None):
+        bits = self.cube.bits
+        flip = lambda bit, other: 1 - bit if other else bit
+        start, size = flip(bits[0], core) * (D // 2), D // 2
+        if axis is not None:
+            size = D // 8
+            start = start + (axis - 1) * (D // 4) + flip(bits[axis], far) * size
+            if further is not None:
+                size = D // 16
+                start = start + flip(bits[3 - axis], further) * size
+        return pl.ds(pl.multiple_of(start, D // 16), size)
+
+    def all(self, rows):
+        return self.panels.at[pl.ds(self.first, 4), rows, :]
+
+    def moves(self, step):
+        cube = self.cube
+        near = lambda code: {"seq": cube.other(code)}
+        if step == 1:
+            return [(near(1), self.all(self.rows(core=1)), self.pair, 0)]
+        if step == 2:
+            return [
+                (near(2 * axis), self.all(self.rows(axis=axis, far=1)), self.flat.at[axis - 1], axis)
+                for axis in (1, 2)
+            ]
+        if step == 3:
+            return [
+                (
+                    near(6 - 2 * axis),
+                    self.all(self.rows(axis=axis, further=1)),
+                    self.edge.at[axis - 1],
+                    2 + axis,
+                )
+                for axis in (1, 2)
+            ]
+        if step == 4:
+            return [
+                (
+                    {"batch": cube.plane(k)},
+                    self.leave.at[k - 1, axis - 1],
+                    self.deep.at[k - 1, axis - 1],
+                    3 + 2 * k + axis - 1,
+                )
+                for k in range(1, cube.levels)
+                for axis in (1, 2)
+            ]
+        if step == 5:
+            there = self.first + cube.level
+            return [
+                (
+                    {"batch": cube.plane(k)},
+                    self.panels.at[there, self.rows(axis=axis, further=0), :],
+                    self.panels.at[there, self.rows(axis=axis, further=0), :],
+                    9 + 2 * k + axis - 1,
+                )
+                for k in range(1, cube.levels)
+                for axis in (1, 2)
+            ]
+        if step == 6:
+            parts = [(6 - 2 * axis, self.all(self.rows(axis=axis, further=0)), 16 + axis) for axis in (1, 2)]
+        elif step == 7:
+            parts = [(2 * axis, self.all(self.rows(axis=axis)), 18 + axis) for axis in (1, 2)]
+        else:
+            parts = [(1, self.all(self.rows()), 21)]
+        return [(near(code), part, part, index) for code, part, index in parts]
+
+    def add(self, rows, found):
+        def one(i, carry):
+            there = self.first + i
+            total = self.panels[there, rows, :].astype(F32) + found[i].astype(F32)
+            self.panels[there, rows, :] = total.astype(BF)
+            return carry
+
+        lax.fori_loop(0, 4, one, 0)
+
+    def take(self, step):
+        if step == 1:
+            self.add(self.rows(), self.pair)
+        elif step == 2:
+            for axis in (1, 2):
+                self.add(self.rows(axis=axis), self.flat.at[axis - 1])
+        elif step == 3:
+            for axis in (1, 2):
+                self.add(self.rows(axis=axis, further=0), self.edge.at[axis - 1])
+        elif step == 4:
+            there = self.first + self.cube.level
+            for axis in (1, 2):
+                rows = self.rows(axis=axis, further=0)
+                total = self.panels[there, rows, :].astype(F32)
+                for k in range(self.cube.levels - 1):
+                    total = total + self.deep[k, axis - 1].astype(F32)
+                self.panels[there, rows, :] = total.astype(BF)
+
+
+class Scatter(Steps):
+    def __init__(self, cube, block, spare, send_sem, recv_sem):
+        self.cube, self.block, self.spare = cube, block, spare
+        self.send_sem, self.recv_sem = send_sem, recv_sem
+
+    def at(self, code, part):
+        return self.block(2 * self.cube.other(code) + part)
+
+    def moves(self, step):
+        near = lambda code: {"seq": self.cube.other(code)}
+        if step == 1:
+            parts = [(1, 2 * i + 1, part, 2 * i + part) for i in range(4) for part in range(2)]
+        elif step == 2:
+            parts = [(2, 2, 0, 8), (2, 6, 0, 9), (4, 4, 1, 10), (4, 6, 1, 11)]
+        else:
+            parts = [(4, 4, 0, 12), (2, 2, 1, 13)]
+        return [(near(to), self.at(code, part), self.spare(k), k) for to, code, part, k in parts]
+
+    def take(self, step):
+        if step == 1:
+            parts = [(2 * i, part, 2 * i + part) for i in range(4) for part in range(2)]
+        else:
+            parts = [(0, 0, 8), (4, 0, 9), (0, 1, 10), (2, 1, 11)]
+        for code, part, k in parts:
+            here = self.at(code, part)
+            here[...] = (here[...].astype(F32) + self.spare(k)[...].astype(F32)).astype(BF)
+
+    def result(self, part):
+        return self.at(0, part)[...].astype(F32) + self.spare(12 + part)[...].astype(F32)
+
+
+class Small(Steps):
+    def __init__(self, cube, array, spare, planes, send_sem, recv_sem):
+        self.cube, self.array, self.spare, self.planes = cube, array, spare, planes
+        self.send_sem, self.recv_sem = send_sem, recv_sem
+
+    def moves(self, step):
+        cube = self.cube
+        if step < 4:
+            return [({"seq": cube.other(1 << (step - 1))}, self.array, self.spare.at[step - 1], step - 1)]
+        here = self.planes.at[cube.level]
+        return [
+            ({"batch": cube.plane(k)}, here, here, 2 + k) for k in range(1, cube.levels)
+        ]
+
+    def take(self, step):
+        if step < 4:
+            self.array[...] += self.spare[step - 1]
+        if step == 3:
+            self.planes[self.cube.level] = self.array[...]
+        if step == 4:
+            total = self.planes[0]
+            for k in range(1, self.cube.levels):
+                total = total + self.planes[k]
+            self.array[...] = total
+
+
+class Gather:
+    def __init__(self, cube, own, slot_ref, send_sem, recv_sem):
+        self.cube, self.own, self.slot_ref = cube, own, slot_ref
+        self.send_sem, self.recv_sem = send_sem, recv_sem
+        self.sent = []
+
+    def push(self, step, code, part):
+        slot = 2 * self.cube.other(code) + part
+        target = self.slot_ref(slot)
+        source = self.own.at[part] if code == 0 else target
+        self.sent.append(
+            self.cube.send(
+                step,
+                source,
+                target,
+                self.send_sem.at[len(self.sent)],
+                self.recv_sem.at[2 * (code ^ step) + part],
+            )
+        )
+
+    def take(self, code, part):
+        slot = self.slot_ref(2 * self.cube.other(code) + part)
+        pltpu.make_async_remote_copy(
+            src_ref=slot,
+            dst_ref=slot,
+            send_sem=self.send_sem.at[0],
+            recv_sem=self.recv_sem.at[2 * code + part],
+            device_id={"seq": self.cube.other(1)},
+            device_id_type=MESH,
+        ).wait_recv()
+
+    def arrived(self, code):
+        for part in range(2):
+            self.take(code, part)
+
+    def open(self):
+        for step, part in ((2, 0), (4, 1), (2, 1), (4, 0), (1, 0), (1, 1)):
+            self.push(step, 0, part)
+
+    def pass_on(self):
+        self.take(2, 0)
+        self.push(4, 2, 0)
+        self.take(4, 1)
+        self.push(2, 4, 1)
+        self.push(1, 2, 0)
+        self.push(1, 4, 1)
+        self.take(2, 1)
+        self.push(1, 2, 1)
+        self.take(4, 0)
+        self.push(1, 4, 0)
+
+    def finish(self):
+        for part in range(2):
+            self.take(6, part)
+            self.push(1, 6, part)
+
+    def close(self):
+        for copy in self.sent:
+            copy.wait_send()
+
+
+def publish_kernel(grads, dvec, *refs):
+    kept, outs, (narrow, broad, load_sem, store_sem, keep_sem) = refs[:3], refs[3:-5], refs[-5:]
+    keeps = [pltpu.make_async_copy(kept[i], outs[24 + i], keep_sem.at[i]) for i in range(3)]
+    order = list(range(8, 16)) + list(range(4, 8)) + list(range(4))
+    loads = [pltpu.make_async_copy(grads.at[i], narrow.at[i], load_sem.at[i]) for i in order]
+    for load in loads + keeps:
+        load.start()
+    for i in range(13):
+        outs[10 + i][...] = dvec[i, :]
+    for i in range(4):
+        outs[23][i * D : (i + 1) * D] = dvec[13 + i, :]
+    stores = []
+    for load, i in zip(loads, order):
+        load.wait()
+        broad[i] = narrow[i].astype(F32)
+        if i < 8:
+            target = outs[i]
+        elif i % 2 == 0:
+            target = outs[8].at[:, pl.ds((i - 8) // 2 * D, D)]
+        else:
+            target = outs[9].at[pl.ds((i - 8) // 2 * D, D), :]
+        store = pltpu.make_async_copy(broad.at[i], target, store_sem.at[i])
+        store.start()
+        stores.append(store)
+    for store in stores + keeps:
+        store.wait()
+
+
+def publish(grads, dvec, kept):
+    vmem = pl.BlockSpec(memory_space=pltpu.VMEM)
+    hbm = pl.BlockSpec(memory_space=pl.ANY)
+    shapes = [(D, D)] * 8 + [(D, 4 * D), (4 * D, D)] + [(D,)] * 13 + [(4 * D,)]
+    return pl.pallas_call(
+        publish_kernel,
+        out_shape=tuple(
+            [jax.ShapeDtypeStruct(shape, F32) for shape in shapes]
+            + [jax.ShapeDtypeStruct(array.shape, array.dtype) for array in kept]
+        ),
+        in_specs=[hbm, vmem] + [hbm] * 3,
+        out_specs=tuple([hbm] * 10 + [vmem] * 14 + [hbm] * 3),
+        scratch_shapes=[
+            pltpu.VMEM((16, D, D), BF),
+            pltpu.VMEM((16, D, D), F32),
+            pltpu.SemaphoreType.DMA((16,)),
+            pltpu.SemaphoreType.DMA((16,)),
+            pltpu.SemaphoreType.DMA((3,)),
+        ],
+        compiler_params=pltpu.CompilerParams(vmem_limit_bytes=48 << 20),
+    )(grads, dvec, *kept)
+
+
+def layer_kernel(
+    sizes,
+    tlen,
+    slen,
+    tord,
+    sord,
+    own,
+    cot,
+    own_memory,
+    vectors,
+    w_small,
+    w_in,
+    w_out,
+    result,
+    dinputs,
+    dmemory,
+    dvec,
+    grads,
+    vec,
+    nrm,
+    memory,
+    stream,
+    weight,
+    kv,
+    queries,
+    ckeys,
+    cvalues,
+    scores,
+    powers,
+    cpowers,
+    inverses,
+    cinverses,
+    mixed,
+    heard,
+    unit,
+    low,
+    tinv,
+    sinv,
+    pairs,
+    flats,
+    edges,
+    deeps,
+    leaves,
+    spares,
+    planes,
+    sem,
+    send_sem,
+    recv_sem,
+    group_send,
+    group_recv,
+    group_sent,
+    scatter_send,
+    scatter_recv,
+    small_send,
+    small_recv,
+    ready,
+):
+    rows, blocks, half, sblocks, shalf, ndoc, window = (
+        sizes["rows"],
+        sizes["blocks"],
+        sizes["half"],
+        sizes["sblocks"],
+        sizes["shalf"],
+        sizes["ndoc"],
+        sizes["window"],
+    )
+    around = -(-window // half)
+    pad = around * half - window
+    sources = sblocks * shalf
+    later = dinputs
+    me = lax.axis_index("seq")
+    scale = float(HDIM) ** -0.5
+    thirds = half // PIECE
+    cube = Cube(me, lax.axis_index("batch"), sizes["levels"])
+    cube.greet()
+
+    def raw(slot):
+        return powers.at[lax.rem(slot, 4), pl.ds(lax.div(slot, 4) * thirds, thirds), :, 0:D]
+
+    def raw_memory(slot):
+        return memory.at[slot]
+
+    gather_rows = Gather(cube, own, raw, send_sem.at[0], recv_sem.at[0])
+    gather_sources = Gather(cube, own_memory, raw_memory, send_sem.at[1], recv_sem.at[1])
+    gather_rows.open()
+    groups = [
+        Reduce(
+            cube, weight, first, pairs.at[turn % 2], flats.at[turn % 2], edges.at[turn % 2],
+            deeps.at[turn % 2], leaves.at[turn % 2], group_send.at[turn], group_recv.at[turn],
+            group_sent.at[turn],
+        )
+        for turn, first in enumerate((8, 12, 4, 0))
+    ]
+
+    def spare_block(k):
+        return powers.at[k % 4, pl.ds(k // 4 * thirds, thirds), :, 0:D]
+
+    rows_back = Scatter(
+        cube, lambda slot: nrm.at[slot], spare_block, scatter_send.at[0], scatter_recv.at[0]
+    )
+    memory_back = Scatter(
+        cube,
+        lambda slot: cvalues.at[pl.ds(pl.multiple_of(slot * shalf, shalf), shalf), :],
+        lambda k: memory.at[k],
+        scatter_send.at[1],
+        scatter_recv.at[1],
+    )
+    small = Small(cube, dvec, spares, planes, small_send, small_recv)
+
+    row = 0
+    for vector_ref in vectors:
+        for start in range(0, vector_ref.shape[0], D):
+            vec[row : row + 1, :] = vector_ref[start : start + D].astype(F32).reshape(1, D)
+            row += 1
+
+    copies = []
+    for index, (source, target) in enumerate(
+        [(w_small[i], weight.at[i]) for i in range(8)]
+        + [(w_in.at[:, pl.ds(D * i, D)], weight.at[8 + 2 * i]) for i in range(4)]
+        + [(w_out.at[pl.ds(D * i, D), :], weight.at[9 + 2 * i]) for i in range(4)]
+    ):
+        copy = pltpu.make_async_copy(source, target, sem.at[index])
+        copy.start()
+        copies.append(copy)
+
+    for order, inverse_of, count in ((tord, tinv, blocks), (sord, sinv, sblocks)):
+        for t in range(count):
+            found = jnp.int32(0)
+            for s in range(count):
+                found = jnp.where(order[0, s] == t, s, found)
+            inverse_of[t] = found
+    tends, sends = [], []
+    tend, send = jnp.int32(0), jnp.int32(0)
+    for d in range(ndoc):
+        tend, send = tend + tlen[0, d], send + slen[0, d]
+        tends.append(tend)
+        sends.append(send)
+    base = [tord[0, 2 * me + b] for b in range(2)]
+
+    def vector(index):
+        return vec[index : index + 1, :]
+
+    for copy in copies:
+        copy.wait()
+
+    states = own[...].reshape(rows, D)
+    own_normed = (centred(states.astype(F32))[0] * vector(0) + vector(1)).astype(BF)
+    queries[...] = ((nn(own_normed, weight[0]) + vector(2)) * scale).astype(BF)
+
+    def project_block(s, block):
+        found, _ = centred(block.astype(F32))
+        normed = (found * vector(0) + vector(1)).astype(BF)
+        nrm[s] = normed.reshape(thirds, PIECE, D)
+        keys = nn(normed, weight[1]).astype(BF)
+        values = (nn(normed, weight[2]) + vector(3)).astype(BF)
+        for quad in range(2):
+            kv[0, quad, s] = keys[:, quad * 256 : (quad + 1) * 256]
+            kv[1, quad, s] = values[:, quad * 256 : (quad + 1) * 256]
+
+    def project(code):
+        def one(part, carry):
+            s = 2 * cube.other(code) + part
+            project_block(s, raw(s)[...].reshape(half, D))
+            return carry
+
+        lax.fori_loop(0, 2, one, 0)
+
+    for part in range(2):
+        project_block(2 * me + part, own[part].reshape(half, D))
+    gather_rows.arrived(1)
+    project(1)
+    gather_rows.pass_on()
+    gather_sources.open()
+    project(2)
+    project(4)
+    gather_rows.arrived(3)
+    project(3)
+    gather_rows.arrived(5)
+    project(5)
+    gather_rows.finish()
+    project(6)
+    gather_rows.arrived(7)
+    project(7)
+    gather_rows.close()
+    gather_sources.pass_on()
+
+    def limits(b):
+        index = lax.broadcasted_iota(jnp.int32, (1, 4 * half), 1)
+        row = index
+        for h in range(1, 4):
+            row = jnp.where(index >= h * half, index - h * half, row)
+        position = base[b] * half + row
+        start = jnp.zeros_like(position)
+        for end in tends:
+            start = jnp.where(position >= end, end, start)
+        shift = (base[b] + 1) * half - window
+        return start - shift, position - shift + 1
+
+    kwin, vwin = [
+        cpowers.at[kind, pl.ds(0, window // PIECE), :, pl.ds(D, 4 * HDIM)] for kind in range(2)
+    ]
+
+    def fill(b, quad):
+        skip = pad // PIECE
+        for j in range(around):
+            slot = tinv[jnp.maximum(base[b] - (around - 1) + j, 0)]
+            for kind, target in ((0, kwin), (1, vwin)):
+                block = kv[kind, quad, slot].reshape(thirds, PIECE, 4 * HDIM)
+                if j == 0:
+                    target[0 : thirds - skip] = block[skip:]
+                else:
+                    target[j * thirds - skip : (j + 1) * thirds - skip] = block
+
+    for b in range(2):
+        begin, stop = limits(b)
+
+        def forward(quad, carry, b=b, begin=begin, stop=stop):
+            fill(b, quad)
+            lanes = pl.ds(pl.multiple_of(quad * 256, 256), 256)
+            block = queries[b * half : (b + 1) * half, lanes].astype(F32)
+            out, inverse = attend(
+                spread_heads(block, 4).astype(BF),
+                kwin,
+                vwin,
+                begin,
+                stop,
+                scores.at[pl.ds(0, window), :],
+                powers.at[b * 2 + quad],
+            )
+            inverses[b * 2 + quad] = jnp.broadcast_to(inverse, (8, 4 * half))
+            mixed[b * half : (b + 1) * half, lanes] = join_heads(out, 4)
+            return carry
+
+        lax.fori_loop(0, 2, forward, 0)
+
+    middle = own[...].reshape(rows, D).astype(F32) + nn(mixed[...].astype(BF), weight[3]) + vector(4)
+    found, spread = centred(middle)
+    later[...] = middle
+    unit[0] = found
+    low[0] = (found * vector(5) + vector(6)).astype(BF)
+    cross_spread = spread
+    low[1] = ((nn(low[0], weight[4]) + vector(7)) * scale).astype(BF)
+
+    gather_sources.finish()
+    for code in (1, 3, 5, 7):
+        gather_sources.arrived(code)
+    for part in range(2):
+        memory[2 * me + part] = own_memory[part]
+    gather_sources.close()
+
+    def place(t, carry):
+        stream[t] = memory[sinv[t]]
+        return carry
+
+    lax.fori_loop(0, sblocks, place, 0)
+    step = sources // 2
+    some = sblocks // 2
+
+    def sources_of(c, carry):
+        part = pl.ds(pl.multiple_of(c * step, step), step)
+        block = stream[pl.ds(c * some, some)].reshape(step, D)
+        ckeys[part, :] = nn(block, weight[5]).astype(BF)
+        cvalues[part, :] = (nn(block, weight[6]) + vector(8)).astype(BF)
+        return carry
+
+    lax.fori_loop(0, sources // step, sources_of, 0)
+    index = lax.broadcasted_iota(jnp.int32, (1, 2 * rows), 1)
+    row = jnp.where(index >= rows, index - rows, index)
+    position = jnp.where(row >= half, base[1] * half + row - half, base[0] * half + row)
+    begin = jnp.zeros_like(position)
+    stop = jnp.full_like(position, sources)
+    for end, send in zip(tends, sends):
+        begin = jnp.where(position >= end, send, begin)
+    for end, send in reversed(list(zip(tends, sends))):
+        stop = jnp.where(position < end, send, stop)
+
+    def cross_forward(pair, carry):
+        lanes = pl.ds(pl.multiple_of(pair * 128, 128), 128)
+        out, inverse = attend(
+            spread_heads(low[1, :, lanes].astype(F32), 2).astype(BF),
+            ckeys.at[:, lanes],
+            cvalues.at[:, lanes],
+            begin,
+            stop,
+            scores,
+            cpowers.at[pair],
+        )
+        cinverses[pair] = jnp.broadcast_to(inverse, (8, 2 * rows))
+        heard[:, lanes] = join_heads(out, 2)
+        return carry
+
+    lax.fori_loop(0, 4, cross_forward, 0)
+    after_cross = later[...] + nn(heard[...].astype(BF), weight[7]) + vector(9)
+    found, spread = centred(after_cross)
+    unit[1] = found
+    final_spread = spread
+    low[2] = (found * vector(10) + vector(11)).astype(BF)
+    later[...] = after_cross + vector(12)
+
+    cotangent = cot[...]
+    unit[2] = jnp.zeros((rows, D), F32)
+
+    def feed(c, carry):
+        fed = low[2]
+        first, second = weight[8 + 2 * c], weight[9 + 2 * c]
+        before = nn(fed, first) + vec[pl.ds(13 + c, 1), :]
+        cumulative = 0.5 * (1.0 + lax.erf(before * (2.0**-0.5)))
+        after = (before * cumulative).astype(BF)
+        slope = cumulative + before * jnp.exp(-0.5 * before * before) * ((2.0 * math.pi) ** -0.5)
+        later[...] += nn(after, second)
+        change = nt(cotangent, second) * slope
+        change_low = change.astype(BF)
+        dvec[pl.ds(13 + c, 1), :] = column_sum(change_low.astype(F32))
+        unit[2] += nt(change_low, first)
+        weight[8 + 2 * c] = tn(fed, change_low).astype(BF)
+        weight[9 + 2 * c] = tn(after, cotangent).astype(BF)
+
+        @pl.when(c == 1)
+        def _():
+            groups[0].begin(1)
+
+        return carry
+
+    lax.fori_loop(0, 4, feed, 0)
+    groups[0].advance(1)
+    groups[1].begin(1)
+    result[...] = later[...].astype(BF)
+    cot_f = cotangent.astype(F32)
+    dvec[12:13, :] = column_sum(cot_f)
+    dfed = unit[2]
+    dvec[10:11, :] = column_sum(dfed * unit[1])
+    dvec[11:12, :] = column_sum(dfed)
+    dlater = cot_f + norm_back(dfed, unit[1], final_spread, vector(10))
+    later[...] = dlater
+    branch = dlater.astype(BF)
+    dvec[9:10, :] = column_sum(branch.astype(F32))
+    dheard = nt(branch, weight[7]).astype(BF)
+    weight[7] = tn(heard[...].astype(BF), branch).astype(BF)
+    low[2] = dheard
+    heard[...] = heard[...] * dheard.astype(F32)
+
+    def cross_backward(pair, carry):
+        lanes = pl.ds(pl.multiple_of(pair * 128, 128), 128)
+
+        def store(c, dkeys, dvalues):
+            part = pl.ds(pl.multiple_of(c * dkeys.shape[0], dkeys.shape[0]), dkeys.shape[0])
+            scores[part, 0:128] = dkeys
+            cvalues[part, lanes] = dvalues.astype(BF)
+
+        out = attend_back(
+            spread_heads(low[1, :, lanes].astype(F32), 2).astype(BF),
+            spread_heads(low[2, :, lanes].astype(F32), 2).astype(BF),
+            spread_heads(heard[:, lanes], 2),
+            ckeys.at[:, lanes],
+            cvalues.at[:, lanes],
+            cinverses[pair, 0:1, :],
+            cpowers.at[pair],
+            store,
+        )
+        ckeys[:, lanes] = scores[:, 0:128].astype(BF)
+        unit[1, :, lanes] = join_heads(out, 2)
+
+        @pl.when(pair == 0)
+        def _():
+            groups[1].advance(1)
+
+        @pl.when(pair == 1)
+        def _():
+            groups[0].advance(2)
+
+        @pl.when(pair == 2)
+        def _():
+            groups[0].advance(3)
+            groups[1].advance(2)
+
+        return carry
+
+    lax.fori_loop(0, 4, cross_backward, 0)
+
+    dvec[8:9, :] = column_sum(cvalues[...].astype(F32))
+    block = stream[...].reshape(sources, D)
+    fresh = [tn(block, ckeys[...]).astype(BF), tn(block, cvalues[...]).astype(BF)]
+
+    def sources_back(c, carry):
+        part = pl.ds(pl.multiple_of(c * step, step), step)
+        back = nt(ckeys[part, :], weight[5]) + nt(cvalues[part, :], weight[6])
+        stream[pl.ds(c * some, some)] = back.astype(BF).reshape(some, shalf, D)
+        return carry
+
+    lax.fori_loop(0, sources // step, sources_back, 0)
+    weight[5] = fresh[0]
+    weight[6] = fresh[1]
+
+    def place_back(s, carry):
+        there = pl.ds(pl.multiple_of(s * shalf, shalf), shalf)
+        cvalues[there, :] = stream[sord[0, s]]
+        return carry
+
+    lax.fori_loop(0, sblocks, place_back, 0)
+    memory_back.begin(1)
+    groups[0].advance(4)
+    groups[1].advance(3)
+    ckeys[0:D, :] = weight[1]
+    ckeys[D : 2 * D, :] = weight[2]
+
+    dcq = unit[1].astype(BF)
+    dvec[7:8, :] = column_sum(dcq.astype(F32)) * scale
+    dcrossed = nt(dcq, weight[4]) * scale
+    weight[4] = (tn(low[0], dcq) * scale).astype(BF)
+    dvec[5:6, :] = column_sum(dcrossed * unit[0])
+    dvec[6:7, :] = column_sum(dcrossed)
+    groups[2].begin(1)
+    dmid = later[...] + norm_back(dcrossed, unit[0], cross_spread, vector(5))
+    later[...] = dmid
+    branch = dmid.astype(BF)
+    dvec[4:5, :] = column_sum(branch.astype(F32))
+    dmixed = nt(branch, weight[3]).astype(BF)
+    weight[3] = tn(mixed[...].astype(BF), branch).astype(BF)
+    low[2] = dmixed
+    mixed[...] = mixed[...] * dmixed.astype(F32)
+
+    for b in range(2):
+        for kind in range(2):
+            if pad:
+                cpowers[2 * kind + b, 0 : pad // PIECE, :, 0:D] = jnp.zeros((pad // PIECE, PIECE, D), BF)
+
+        def backward(quad, carry, b=b):
+            fill(b, quad)
+            lanes = pl.ds(pl.multiple_of(quad * 256, 256), 256)
+
+            def store(c, dkeys, dvalues):
+                pieces = dkeys.shape[0] // PIECE
+                part = pl.ds(c * pieces + pad // PIECE, pieces)
+                cpowers[b, part, :, lanes] = dkeys.astype(BF).reshape(pieces, PIECE, 256)
+                cpowers[2 + b, part, :, lanes] = dvalues.astype(BF).reshape(pieces, PIECE, 256)
+
+            out = attend_back(
+                spread_heads(queries[b * half : (b + 1) * half, lanes].astype(F32), 4).astype(BF),
+                spread_heads(low[2, b * half : (b + 1) * half, lanes].astype(F32), 4).astype(BF),
+                spread_heads(mixed[b * half : (b + 1) * half, lanes], 4),
+                kwin,
+                vwin,
+                inverses[b * 2 + quad, 0:1, :],
+                powers.at[b * 2 + quad],
+                store,
+            )
+            unit[1, b * half : (b + 1) * half, lanes] = join_heads(out, 4)
+
+            @pl.when(quad == 0)
+            def _():
+                if b == 0:
+                    groups[0].advance(5)
+                    groups[1].advance(4)
+                    groups[2].advance(1)
+                    memory_back.advance(1)
+                else:
+                    groups[1].advance(6)
+                    memory_back.advance(2)
+                    groups[2].advance(2)
+
+            return carry
+
+        lax.fori_loop(0, 2, backward, 0)
+        if b == 0:
+            groups[0].advance(6)
+            groups[1].advance(5)
+    for axis in (1, 2):
+        pl.semaphore_signal(
+            ready.at[axis - 1],
+            inc=1,
+            device_id={"seq": cube.other(2 * axis)},
+            device_id_type=MESH,
+        )
+    groups[0].advance(7)
+    groups[2].advance(3)
+
+    dq = unit[1].astype(BF)
+    dvec[2:3, :] = column_sum(dq.astype(F32)) * scale
+    heard[...] = nt(dq, weight[0]) * scale
+    own_normed = nrm[pl.ds(2 * me, 2)].reshape(rows, D)
+    weight[0] = (tn(own_normed, dq) * scale).astype(BF)
+
+    def assemble(s, carry):
+        for kind in range(2):
+            for third in range(thirds):
+                total = jnp.zeros((PIECE, D), F32)
+                for b in range(2):
+                    back = base[b] - tord[0, s]
+                    inside = (back >= 0) & (back < around)
+                    first = jnp.clip(around - 1 - back, 0, around - 1) * thirds
+                    part = cpowers[2 * kind + b, first + third][:, 0:D]
+                    total = total + jnp.where(inside, part.astype(F32), 0.0)
+                total_low = total.astype(BF)
+                if kind == 1:
+                    dvec[3:4, :] += column_sum(total_low.astype(F32))
+                for quad in range(2):
+                    kv[kind, quad, s, third * PIECE : (third + 1) * PIECE, :] = total_low[
+                        :, quad * 256 : (quad + 1) * 256
+                    ]
+        return carry
+
+    dvec[3:4, :] = jnp.zeros((1, D), F32)
+    lax.fori_loop(0, blocks, assemble, 0)
+    whole = nrm[...].reshape(blocks * half, D)
+    for kind in range(2):
+        for quad in range(2):
+            weight[1 + kind, :, quad * 256 : (quad + 1) * 256] = tn(
+                whole, kv[kind, quad].reshape(blocks * half, 256)
+            ).astype(BF)
+    groups[3].begin(1)
+    memory_back.end(3)
+    for part in range(2):
+        dmemory[part * shalf : (part + 1) * shalf, :] = memory_back.result(part)
+    groups[1].advance(7)
+    groups[2].advance(4)
+
+    def spread_back(code):
+        def one(part, carry):
+            s = 2 * cube.other(code) + part
+            total = jnp.zeros((half, D), F32)
+            for kind in range(2):
+                for quad in range(2):
+                    total = total + nt(
+                        kv[kind, quad, s],
+                        ckeys[kind * D : (kind + 1) * D, quad * 256 : (quad + 1) * 256],
+                    )
+            if code == 0:
+                total = total + heard[pl.ds(pl.multiple_of(part * half, half), half), :]
+            nrm[s] = total.astype(BF).reshape(thirds, PIECE, D)
+            return carry
+
+        lax.fori_loop(0, 2, one, 0)
+
+    for code in (1, 3, 5, 7):
+        spread_back(code)
+    groups[3].advance(1)
+    rows_back.begin(1)
+    for code in (6, 2, 4, 0):
+        spread_back(code)
+    groups[2].advance(5)
+    for axis in (1, 2):
+        pl.semaphore_wait(ready.at[axis - 1], 1)
+    rows_back.advance(1)
+    groups[3].advance(2)
+    rows_back.advance(2)
+    groups[2].advance(6)
+    groups[3].advance(3)
+    rows_back.end(3)
+    dvec[0:2, :] = jnp.zeros((2, D), F32)
+    dvec[17:VECTORS, :] = jnp.zeros((VECTORS - 17, D), F32)
+    for part in range(2):
+        own_unit, own_spread = centred(own[part].reshape(half, D).astype(F32))
+        dnormed = rows_back.result(part).reshape(half, D)
+        here = pl.ds(part * half, half)
+        dinputs[here, :] = later[here, :] + norm_back(dnormed, own_unit, own_spread, vector(0))
+        dvec[0:1, :] += column_sum(dnormed * own_unit)
+        dvec[1:2, :] += column_sum(dnormed)
+    small.begin(1)
+    groups[3].advance(4)
+    groups[2].advance(7)
+    small.advance(1)
+    groups[3].advance(5)
+    small.advance(2)
+    groups[3].advance(6)
+    small.advance(3)
+    groups[0].end(8)
+    groups[1].end(8)
+    groups[2].end(8)
+    copies = [
+        pltpu.make_async_copy(
+            weight.at[pl.ds(first, size)], grads.at[pl.ds(first, size)], sem.at[first]
+        )
+        for first, size in ((4, 12), (0, 4))
+    ]
+    copies[0].start()
+    small.end(4)
+    small.take(4)
+    groups[3].advance(7)
+    groups[3].end(8)
+    copies[1].start()
+    for copy in copies:
+        copy.wait()
+
+
+def layer_call(sizes, small_ints, own, cot, own_memory, vectors, w_small, w_in, w_out):
+    rows, blocks, half, sblocks, shalf, window = (
+        sizes["rows"],
+        sizes["blocks"],
+        sizes["half"],
+        sizes["sblocks"],
+        sizes["shalf"],
+        sizes["window"],
+    )
+    sources = sblocks * shalf
+    levels = sizes["levels"]
+    vmem = pl.BlockSpec(memory_space=pltpu.VMEM)
+    smem = pl.BlockSpec(memory_space=pltpu.SMEM)
+    hbm = pl.BlockSpec(memory_space=pl.ANY)
+
+    count = len(vectors)
+
+    def body(*refs):
+        head, rest = refs[:7], refs[7:]
+        vector_refs, rest = rest[:count], rest[count:]
+        layer_kernel(sizes, *head, vector_refs, rest[:8], *rest[8:])
+
+    return pl.pallas_call(
+        body,
+        out_shape=(
+            jax.ShapeDtypeStruct((rows, D), BF),
+            jax.ShapeDtypeStruct((rows, D), F32),
+            jax.ShapeDtypeStruct((2 * shalf, D), F32),
+            jax.ShapeDtypeStruct((VECTORS, D), F32),
+            jax.ShapeDtypeStruct((16, D, D), BF),
+        ),
+        in_specs=[smem] * 4 + [vmem] * (3 + count) + [hbm] * 10,
+        out_specs=(vmem, vmem, vmem, vmem, hbm),
+        scratch_shapes=[
+            pltpu.VMEM((VECTORS, D), F32),
+            pltpu.VMEM((blocks, half // PIECE, PIECE, D), BF),
+            pltpu.VMEM((sblocks, shalf, D), BF),
+            pltpu.VMEM((sblocks, shalf, D), BF),
+            pltpu.VMEM((16, D, D), BF),
+            pltpu.VMEM((2, 2, blocks, half, 256), BF),
+            pltpu.VMEM((rows, D), BF),
+            pltpu.VMEM((sources, D), BF),
+            pltpu.VMEM((sources, D), BF),
+            pltpu.VMEM((sources, 2 * rows), F32),
+            pltpu.VMEM((4, window // PIECE, PIECE, 4 * half), BF),
+            pltpu.VMEM((4, sources // PIECE, PIECE, 2 * rows), BF),
+            pltpu.VMEM((4, 8, 4 * half), F32),
+            pltpu.VMEM((4, 8, 2 * rows), F32),
+            pltpu.VMEM((rows, D), F32),
+            pltpu.VMEM((rows, D), F32),
+            pltpu.VMEM((3, rows, D), F32),
+            pltpu.VMEM((3, rows, D), BF),
+            pltpu.SMEM((blocks,), jnp.int32),
+            pltpu.SMEM((sblocks,), jnp.int32),
+            pltpu.VMEM((2, 4, D // 2, D), BF),
+            pltpu.VMEM((2, 2, 4, D // 8, D), BF),
+            pltpu.VMEM((2, 2, 4, D // 16, D), BF),
+            pltpu.VMEM((2, levels - 1, 2, D // 16, D), BF),
+            pltpu.VMEM((2, levels - 1, 2, D // 16, D), BF),
+            pltpu.VMEM((3, VECTORS, D), F32),
+            pltpu.VMEM((levels, VECTORS, D), F32),
+            pltpu.SemaphoreType.DMA((16,)),
+            pltpu.SemaphoreType.DMA((2, 16)),
+            pltpu.SemaphoreType.DMA((2, 16)),
+            pltpu.SemaphoreType.DMA((4, 22)),
+            pltpu.SemaphoreType.DMA((4, 22)),
+            pltpu.SemaphoreType.REGULAR((4, 3)),
+            pltpu.SemaphoreType.DMA((2, 14)),
+            pltpu.SemaphoreType.DMA((2, 14)),
+            pltpu.SemaphoreType.DMA((6,)),
+            pltpu.SemaphoreType.DMA((6,)),
+            pltpu.SemaphoreType.REGULAR((2,)),
+        ],
+        compiler_params=pltpu.CompilerParams(
+            vmem_limit_bytes=64 << 20, collective_id=0, has_side_effects=True
+        ),
+    )(*small_ints, own, cot, own_memory, *vectors, *w_small, w_in, w_out)
+
+
+def fused_on_device(
+    inputs, memory, target_lengths, source_lengths, target_order, source_order,
+    self_gain, self_shift, self_query, query_bias, self_key, self_value, value_bias,
+    self_output, output_bias, cross_gain, cross_shift, cross_query, cquery_bias, cross_key,
+    cross_value, cvalue_bias, cross_output, coutput_bias, final_gain, final_shift,
+    inner_weight, inner_bias, outer_weight, outer_bias, cotangent,
+):
+    rows = inputs.shape[1]
+    blocks = target_order.shape[1]
+    sblocks = source_order.shape[1]
+    ranks = lax.axis_size("seq")
+    half = ranks * rows // blocks
+    shalf = ranks * memory.shape[1] // sblocks
+    ndoc = target_lengths.shape[1]
+    reach = max(LONGEST, blocks * half - LONGEST - SHORTEST * (ndoc - 1))
+    window = -(-(reach - 1 + half) // CHUNK) * CHUNK
+    sizes = dict(
+        rows=rows, blocks=blocks, half=half, sblocks=sblocks, shalf=shalf, ndoc=ndoc, window=window,
+        levels=lax.axis_size("batch"),
+    )
+    result, dinputs, dmemory, dvec, grads = layer_call(
+        sizes, (target_lengths, source_lengths, target_order, source_order),
+        inputs.reshape(2, half // PIECE, PIECE, D), cotangent[0], memory.reshape(2, shalf, D),
+        (
+            self_gain, self_shift, query_bias, value_bias, output_bias, cross_gain, cross_shift,
+            cquery_bias, cvalue_bias, coutput_bias, final_gain, final_shift, outer_bias, inner_bias,
+        ),
+        (self_query, self_key, self_value, self_output, cross_query, cross_key, cross_value, cross_output),
+        inner_weight, outer_weight,
+    )
+    made = publish(grads, dvec, (result, dinputs, dmemory))
+    result, dinputs, dmemory = made[24:]
+    squares, wide, tall, rows_of, units = made[:8], made[8], made[9], made[10:23], made[23]
+    return (
+        result[None], dinputs[None], dmemory[None],
+        rows_of[0], rows_of[1], squares[0], rows_of[2], squares[1], squares[2], rows_of[3],
+        squares[3], rows_of[4], rows_of[5], rows_of[6], squares[4], rows_of[7], squares[5],
+        squares[6], rows_of[8], squares[7], rows_of[9], rows_of[10], rows_of[11],
+        wide, units, tall, rows_of[12],
+    )
+
+
 def solution(mesh):
     in_specs = (
         P("batch", "seq", None),
@@ -447,5 +1635,6 @@
         P(),
     )
     return jax.shard_map(
-        on_device, mesh=mesh, in_specs=in_specs, out_specs=out_specs, check_vma=False
-    )
+        fused_on_device if (mesh.shape["seq"], mesh.shape["batch"]) == (8, 4) else on_device,
+        mesh=mesh, in_specs=in_specs, out_specs=out_specs, check_vma=False,
+    )

time: 915 us -> 206 us (0.23); the launches traced: 903 us -> 206 us
  waiting for transfers between devices: 353 us -> 0 us
  matrix products: 289 us -> 0 us
  Pallas kernels: 0 us -> 201 us
  local copies, waits for them, and re-layouts: 123 us -> 3.91 us
  other arithmetic: 72.6 us -> 0 us
  blocking collectives: 42.4 us -> 0 us
  between operations: 15.6 us -> 0.88 us
    dot_general x79 -> x0, matrix products: 289 us -> none  [the longest x9 46.4 us: block_back(): jnp.einsum('qhk,qhd->khd', weights.astype(jnp.bfloat16), grad_heads, pref...]
    psum x1 -> x0, waiting for transfers between devices: 235 us -> none  [on_device(): lax.psum((self_gain_grad, self_shift_grad, self_query_grad, query_bias_gr...]
    pallas_call x0 -> x2, Pallas kernels: none -> 201 us  [the longest x1 191 us: layer_call(): pl.pallas_call(body, out_shape=(jax.ShapeDtypeStruct((rows, D), BF), jax....]
    unnamed x236 -> x8, local copies, waits for them, and re-layouts: 74.2 us -> 3.91 us
    all_gather x4 -> x0, waiting for transfers between devices: 61.3 us -> none  [the longest x1 32.2 us: on_device(): lax.all_gather(keys, 'seq', axis=0, tiled=True)]
    unnamed x13 -> x0, waiting for transfers between devices: 56.1 us -> none
    reduce_sum x41 -> x0, other arithmetic: 46.1 us -> none  [the longest x2 25.7 us: online(): total = jnp.sum(powers, axis=-1)]
    psum x1 -> x0, blocking collectives: 42.4 us -> none  [on_device(): lax.psum((self_gain_grad, self_shift_grad, self_query_grad, query_bias_gr...]
  transfers between devices with their start and end apart: 9 -> 0, of which waited for: 6 -> 0; matrix products, arithmetic and copies ran while one was open for 33% -> 0% of each run, Pallas kernels for 0% -> 0%
where the time goes in v1:
time: 206 us
  Pallas kernels  201 us (98%)
  local copies, waits for them, and re-layouts  3.91 us (2%)
    pallas_call x1, Pallas kernels, layer_call(): pl.pallas_call(body, out_shape=(jax.ShapeDtypeStruct((rows, D), BF), jax....  191 us
    pallas_call x1, Pallas kernels, publish(): pl.pallas_call(publish_kernel, out_shape=tuple([jax.ShapeDtypeStruct(shap...  9.77 us

profile of v1, /device:TPU:0, one launch (start us, length us, event | category | flops | bytes accessed | tf_op | source)
XLA Modules:
  0.0 205.6 jit_solution(3175361594378609095)
XLA Ops:
  0.7 191.0 %shard_map.502 = (bf16[384,512]{1,0:T(8,128)(2,1)}, f32[384,512]{1,0:T(8,128)}, f32[192,512]{1,0:T(8,128)}, f32[24,512]{1,0:T(8,128)}, bf16[16,512,512]{2,1,0:T(8,128)(2,1)}) custom-call(s32[1,33]{1,0:T(1,128)} %refs_0_.1, s32[1,33]{1,0:T(1,128)} %refs_1_.1, s32[1,16]{1,0:T(1,128)} %refs_2_.1, s32[1,16]{1,0:T(1,128)} %refs_3_.1, ...), custom_call_target="tpu_custom_call" | custom-call | tf_op jit(solution)/shard_map/pallas_call | solution.py:1475
  191.7 0.0 copy-start
  191.7 1.1 copy-done
  192.8 0.0 copy-start.1
  192.8 1.0 copy-done.1
  193.8 0.0 copy-start.2
  193.8 1.0 copy-done.2
  194.8 0.0 copy-start.3
  194.8 0.8 copy-done.3
  195.6 9.8 %shard_map.503 = (f32[512,512]{1,0:T(8,128)}, f32[512,512]{1,0:T(8,128)}, f32[512,512]{1,0:T(8,128)}, f32[512,512]{1,0:T(8,128)}, f32[512,512]{1,0:T(8,128)}, /*...) custom-call(bf16[16,512,512]{2,1,0:T(8,128)(2,1)} %get-tuple-element, ...), custom_call_target="tpu_custom_call" | custom-call | tf_op jit(solution)/shard_map/pallas_call | solution.py:850
Async XLA Ops:
  191.7 1.1 copy-start
  192.8 1.0 copy-start.1
  193.8 1.0 copy-start.2
  194.8 0.8 copy-start.3

commit v2 on v1

--- a/solution.py
+++ b/solution.py
@@ -390,6 +390,25 @@
 LONGEST = 1024
 CHUNK = 256
 PIECE = 64
+
+SCHEDULE = dict(
+    half="A",
+    heard="BA",
+    pair0="B",
+    pair1="A",
+    pair3="AB",
+    sources="BV",
+    middle="CA",
+    self0="CM",
+    self1="BMV",
+    window="AC",
+    self2="B",
+    self3="A",
+    weights="ECME",
+    through0="BC",
+    theirs="R",
+    end="ECMREACAERBECRSESVECSBE",
+)
 MESH = pl.DeviceIdType.MESH
 PARTS = 2
 BF = jnp.bfloat16
@@ -526,7 +545,7 @@
 
     def greet(self):
         barrier = pltpu.get_barrier_semaphore()
-        for code in (1, 2, 4):
+        for code in range(1, 8):
             pl.semaphore_signal(
                 barrier, inc=1, device_id={"seq": self.other(code)}, device_id_type=MESH
             )
@@ -534,7 +553,7 @@
             pl.semaphore_signal(
                 barrier, inc=1, device_id={"batch": self.plane(step)}, device_id_type=MESH
             )
-        pl.semaphore_wait(barrier, 2 + self.levels)
+        pl.semaphore_wait(barrier, 6 + self.levels)
 
     def send(self, code, source, target, send_sem, recv_sem):
         copy = pltpu.make_async_remote_copy(
@@ -571,37 +590,46 @@
         for copy in self.copies(step):
             copy.wait()
 
-    def advance(self, step):
-        self.end(step)
-        self.take(step)
-        self.begin(step + 1)
+    step, last = 0, 0
+
+    def advance(self):
+        if self.step:
+            self.end(self.step)
+            self.take(self.step)
+        self.step += 1
+        if self.step <= self.last:
+            self.begin(self.step)
+
+    def take(self, step):
+        pass
 
 
 class Reduce(Steps):
-    def __init__(self, cube, panels, first, pair, flat, edge, deep, leave, send_sem, recv_sem, sent):
+    last = 8
+
+    def __init__(self, cube, panels, first, pair, flat, edge, deep, leave, send_sem, recv_sem, sent, before, finish):
+        self.before, self.finish, self.freed = before, finish, set()
         self.cube, self.panels, self.first = cube, panels, first
         self.pair, self.flat, self.edge, self.deep, self.leave = pair, flat, edge, deep, leave
         self.send_sem, self.recv_sem, self.sent = send_sem, recv_sem, sent
 
+    def await_free(self, index):
+        if index not in self.freed:
+            self.freed.add(index)
+            pl.semaphore_wait(self.sent.at[index], 1)
+
     def begin(self, step):
         for index in {6: (1, 2), 8: (0,)}.get(step, ()):
-            pl.semaphore_wait(self.sent.at[index], 1)
+            self.await_free(index)
+        if self.before is not None:
+            for index in {1: (0,), 2: (1, 2)}.get(step, ()):
+                self.before.await_free(index)
         if step == 4:
             for k in range(1, self.cube.levels):
                 there = self.first + self.cube.plane(k)
                 for axis in (1, 2):
                     self.leave[k - 1, axis - 1] = self.panels[there, self.rows(axis=axis, further=0), :]
         super().begin(step)
-
-    def end(self, step):
-        super().end(step)
-        for index in {1: (0,), 3: (1, 2)}.get(step, ()):
-            pl.semaphore_signal(
-                self.sent.at[index],
-                inc=1,
-                device_id={"seq": self.cube.other(1 << index)},
-                device_id_type=MESH,
-            )
 
     def rows(self, core=0, axis=None, far=0, further=None):
         bits = self.cube.bits
@@ -695,12 +723,30 @@
                 for k in range(self.cube.levels - 1):
                     total = total + self.deep[k, axis - 1].astype(F32)
                 self.panels[there, rows, :] = total.astype(BF)
+        elif step == 8:
+            self.finish()
+        for index in {1: (0,), 3: (1, 2)}.get(step, ()):
+            pl.semaphore_signal(
+                self.sent.at[index],
+                inc=1,
+                device_id={"seq": self.cube.other(1 << index)},
+                device_id_type=MESH,
+            )
 
 
 class Scatter(Steps):
-    def __init__(self, cube, block, spare, send_sem, recv_sem):
+    last = 3
+
+    def __init__(self, cube, block, spare, send_sem, recv_sem, ready, finish):
         self.cube, self.block, self.spare = cube, block, spare
+        self.ready, self.finish = ready, finish
         self.send_sem, self.recv_sem = send_sem, recv_sem
+
+    def begin(self, step):
+        if self.ready is not None:
+            for index in {1: (0,), 2: (1, 2)}.get(step, ()):
+                pl.semaphore_wait(self.ready.at[index], 1)
+        super().begin(step)
 
     def at(self, code, part):
         return self.block(2 * self.cube.other(code) + part)
@@ -716,6 +762,9 @@
         return [(near(to), self.at(code, part), self.spare(k), k) for to, code, part, k in parts]
 
     def take(self, step):
+        if step == 3:
+            self.finish()
+            return
         if step == 1:
             parts = [(2 * i, part, 2 * i + part) for i in range(4) for part in range(2)]
         else:
@@ -729,28 +778,33 @@
 
 
 class Small(Steps):
-    def __init__(self, cube, array, spare, planes, send_sem, recv_sem):
-        self.cube, self.array, self.spare, self.planes = cube, array, spare, planes
+    last = 2
+
+    def __init__(self, cube, array, near, planes, send_sem, recv_sem):
+        self.cube, self.array, self.near, self.planes = cube, array, near, planes
         self.send_sem, self.recv_sem = send_sem, recv_sem
 
     def moves(self, step):
         cube = self.cube
-        if step < 4:
-            return [({"seq": cube.other(1 << (step - 1))}, self.array, self.spare.at[step - 1], step - 1)]
+        if step == 1:
+            here = self.near.at[cube.me]
+            return [({"seq": cube.other(code)}, here, here, code - 1) for code in range(1, 8)]
         here = self.planes.at[cube.level]
-        return [
-            ({"batch": cube.plane(k)}, here, here, 2 + k) for k in range(1, cube.levels)
-        ]
+        return [({"batch": cube.plane(k)}, here, here, 6 + k) for k in range(1, cube.levels)]
+
+    def begin(self, step):
+        if step == 1:
+            self.near[self.cube.me] = self.array[...]
+        super().begin(step)
 
     def take(self, step):
-        if step < 4:
-            self.array[...] += self.spare[step - 1]
-        if step == 3:
-            self.planes[self.cube.level] = self.array[...]
-        if step == 4:
-            total = self.planes[0]
-            for k in range(1, self.cube.levels):
-                total = total + self.planes[k]
+        found = self.near if step == 1 else self.planes
+        total = found[0]
+        for k in range(1, found.shape[0]):
+            total = total + found[k]
+        if step == 1:
+            self.planes[self.cube.level] = total
+        else:
             self.array[...] = total
 
 
@@ -909,7 +963,7 @@
     edges,
     deeps,
     leaves,
-    spares,
+    nears,
     planes,
     sem,
     send_sem,
@@ -951,20 +1005,43 @@
     gather_rows = Gather(cube, own, raw, send_sem.at[0], recv_sem.at[0])
     gather_sources = Gather(cube, own_memory, raw_memory, send_sem.at[1], recv_sem.at[1])
     gather_rows.open()
-    groups = [
-        Reduce(
-            cube, weight, first, pairs.at[turn % 2], flats.at[turn % 2], edges.at[turn % 2],
-            deeps.at[turn % 2], leaves.at[turn % 2], group_send.at[turn], group_recv.at[turn],
-            group_sent.at[turn],
+    def deliver(turn, first):
+        def go():
+            pltpu.make_async_copy(
+                weight.at[pl.ds(first, 4)], grads.at[pl.ds(first, 4)], sem.at[turn]
+            ).start()
+
+        return go
+
+    groups = []
+    for turn, first in enumerate((8, 12, 4, 0)):
+        groups.append(
+            Reduce(
+                cube, weight, first, pairs.at[turn % 2], flats.at[turn % 2], edges.at[turn % 2],
+                deeps.at[turn % 2], leaves.at[turn % 2], group_send.at[turn], group_recv.at[turn],
+                group_sent.at[turn], groups[turn - 2] if turn > 1 else None, deliver(turn, first),
+            )
         )
-        for turn, first in enumerate((8, 12, 4, 0))
-    ]
 
     def spare_block(k):
         return powers.at[k % 4, pl.ds(k // 4 * thirds, thirds), :, 0:D]
 
+    def end_rows():
+        for part in range(2):
+            own_unit, own_spread = centred(own[part].reshape(half, D).astype(F32))
+            dnormed = rows_back.result(part).reshape(half, D)
+            here = pl.ds(part * half, half)
+            dinputs[here, :] = later[here, :] + norm_back(dnormed, own_unit, own_spread, vector(0))
+            dvec[0:1, :] += column_sum(dnormed * own_unit)
+            dvec[1:2, :] += column_sum(dnormed)
+
+    def end_memory():
+        for part in range(2):
+            dmemory[part * shalf : (part + 1) * shalf, :] = memory_back.result(part)
+
     rows_back = Scatter(
-        cube, lambda slot: nrm.at[slot], spare_block, scatter_send.at[0], scatter_recv.at[0]
+        cube, lambda slot: nrm.at[slot], spare_block, scatter_send.at[0], scatter_recv.at[0],
+        ready, end_rows,
     )
     memory_back = Scatter(
         cube,
@@ -972,9 +1049,29 @@
         lambda k: memory.at[k],
         scatter_send.at[1],
         scatter_recv.at[1],
-    )
-    small = Small(cube, dvec, spares, planes, small_send, small_recv)
-
+        None,
+        end_memory,
+    )
+    smalls = [
+        Small(
+            cube, dvec.at[pl.ds(start, 8 * size), :],
+            nears.at[:, pl.ds(start, 8 * size), :], planes.at[:, pl.ds(start, 8 * size), :],
+            small_send.at[turn], small_recv.at[turn],
+        )
+        for turn, (start, size) in enumerate(((0, 1), (8, 2)))
+    ]
+    exchanges = dict(
+        A=groups[0], B=groups[1], C=groups[2], E=groups[3], R=rows_back, M=memory_back,
+        S=smalls[0], V=smalls[1],
+    )
+    counts = dict(A=9, B=9, C=9, E=9, R=4, M=4, S=3, V=3)
+
+    def pump(point):
+        for name in SCHEDULE.get(point, ""):
+            counts[name] -= 1
+            exchanges[name].advance()
+
+    dvec[...] = jnp.zeros((VECTORS, D), F32)
     row = 0
     for vector_ref in vectors:
         for start in range(0, vector_ref.shape[0], D):
@@ -1185,13 +1282,12 @@
 
         @pl.when(c == 1)
         def _():
-            groups[0].begin(1)
+            pump("half")
 
         return carry
 
     lax.fori_loop(0, 4, feed, 0)
-    groups[0].advance(1)
-    groups[1].begin(1)
+    pump("feed")
     result[...] = later[...].astype(BF)
     cot_f = cotangent.astype(F32)
     dvec[12:13, :] = column_sum(cot_f)
@@ -1206,6 +1302,7 @@
     weight[7] = tn(heard[...].astype(BF), branch).astype(BF)
     low[2] = dheard
     heard[...] = heard[...] * dheard.astype(F32)
+    pump("heard")
 
     def cross_backward(pair, carry):
         lanes = pl.ds(pl.multiple_of(pair * 128, 128), 128)
@@ -1228,18 +1325,11 @@
         ckeys[:, lanes] = scores[:, 0:128].astype(BF)
         unit[1, :, lanes] = join_heads(out, 2)
 
-        @pl.when(pair == 0)
-        def _():
-            groups[1].advance(1)
-
-        @pl.when(pair == 1)
-        def _():
-            groups[0].advance(2)
-
-        @pl.when(pair == 2)
-        def _():
-            groups[0].advance(3)
-            groups[1].advance(2)
+        for index in range(4):
+
+            @pl.when(pair == index)
+            def _(index=index):
+                pump("pair" + str(index))
 
         return carry
 
@@ -1248,6 +1338,8 @@
     dvec[8:9, :] = column_sum(cvalues[...].astype(F32))
     block = stream[...].reshape(sources, D)
     fresh = [tn(block, ckeys[...]).astype(BF), tn(block, cvalues[...]).astype(BF)]
+
+    pump("sums")
 
     def sources_back(c, carry):
         part = pl.ds(pl.multiple_of(c * step, step), step)
@@ -1265,9 +1357,7 @@
         return carry
 
     lax.fori_loop(0, sblocks, place_back, 0)
-    memory_back.begin(1)
-    groups[0].advance(4)
-    groups[1].advance(3)
+    pump("sources")
     ckeys[0:D, :] = weight[1]
     ckeys[D : 2 * D, :] = weight[2]
 
@@ -1277,7 +1367,6 @@
     weight[4] = (tn(low[0], dcq) * scale).astype(BF)
     dvec[5:6, :] = column_sum(dcrossed * unit[0])
     dvec[6:7, :] = column_sum(dcrossed)
-    groups[2].begin(1)
     dmid = later[...] + norm_back(dcrossed, unit[0], cross_spread, vector(5))
     later[...] = dmid
     branch = dmid.astype(BF)
@@ -1286,6 +1375,7 @@
     weight[3] = tn(mixed[...].astype(BF), branch).astype(BF)
     low[2] = dmixed
     mixed[...] = mixed[...] * dmixed.astype(F32)
+    pump("middle")
 
     for b in range(2):
         for kind in range(2):
@@ -1314,33 +1404,40 @@
             )
             unit[1, b * half : (b + 1) * half, lanes] = join_heads(out, 4)
 
-            @pl.when(quad == 0)
-            def _():
-                if b == 0:
-                    groups[0].advance(5)
-                    groups[1].advance(4)
-                    groups[2].advance(1)
-                    memory_back.advance(1)
-                else:
-                    groups[1].advance(6)
-                    memory_back.advance(2)
-                    groups[2].advance(2)
+            for index in range(2):
+
+                @pl.when(quad == index)
+                def _(index=index):
+                    pump("self" + str(2 * b + index))
 
             return carry
 
         lax.fori_loop(0, 2, backward, 0)
+
+        ratio = half // shalf
+        for j in range(around):
+            slot = tinv[jnp.maximum(base[b] - (around - 1) + j, 0)]
+            stream[j * ratio : (j + 1) * ratio] = nrm[slot].reshape(ratio, shalf, D)
+        normed = stream[0 : around * ratio].reshape(around * half, D)
+        for kind in range(2):
+            change = cpowers[2 * kind + b, 0 : around * thirds, :, 0:D].reshape(around * half, D)
+            if kind == 1:
+                dvec[3:4, :] += column_sum(change.astype(F32))
+            total = tn(normed, change)
+            there = slice(kind * D, (kind + 1) * D)
+            if b == 0:
+                scores[there, 0:D] = total
+            else:
+                weight[1 + kind] = (scores[there, 0:D] + total).astype(BF)
         if b == 0:
-            groups[0].advance(6)
-            groups[1].advance(5)
-    for axis in (1, 2):
+            pump("window")
+    for index in range(3):
         pl.semaphore_signal(
-            ready.at[axis - 1],
+            ready.at[index],
             inc=1,
-            device_id={"seq": cube.other(2 * axis)},
+            device_id={"seq": cube.other(1 << index)},
             device_id_type=MESH,
         )
-    groups[0].advance(7)
-    groups[2].advance(3)
 
     dq = unit[1].astype(BF)
     dvec[2:3, :] = column_sum(dq.astype(F32)) * scale
@@ -1348,106 +1445,51 @@
     own_normed = nrm[pl.ds(2 * me, 2)].reshape(rows, D)
     weight[0] = (tn(own_normed, dq) * scale).astype(BF)
 
-    def assemble(s, carry):
-        for kind in range(2):
+    pump("weights")
+
+    for b in range(2):
+
+        def through(c, carry, b=b):
+            part = pl.ds(c * around, around)
+            dkeys = cpowers[b, part, :, 0:D].reshape(around * PIECE, D)
+            dvalues = cpowers[2 + b, part, :, 0:D].reshape(around * PIECE, D)
+            total = nt(dkeys, ckeys[0:D, :]) + nt(dvalues, ckeys[D : 2 * D, :])
+            cpowers[b, part, :, 0:D] = total.astype(BF).reshape(around, PIECE, D)
+            return carry
+
+        lax.fori_loop(0, thirds, through, 0)
+        pump("through" + str(b))
+
+    def assemble(code):
+        def one(part, carry):
+            s = 2 * cube.other(code) + part
             for third in range(thirds):
                 total = jnp.zeros((PIECE, D), F32)
                 for b in range(2):
                     back = base[b] - tord[0, s]
                     inside = (back >= 0) & (back < around)
                     first = jnp.clip(around - 1 - back, 0, around - 1) * thirds
-                    part = cpowers[2 * kind + b, first + third][:, 0:D]
-                    total = total + jnp.where(inside, part.astype(F32), 0.0)
-                total_low = total.astype(BF)
-                if kind == 1:
-                    dvec[3:4, :] += column_sum(total_low.astype(F32))
-                for quad in range(2):
-                    kv[kind, quad, s, third * PIECE : (third + 1) * PIECE, :] = total_low[
-                        :, quad * 256 : (quad + 1) * 256
-                    ]
-        return carry
-
-    dvec[3:4, :] = jnp.zeros((1, D), F32)
-    lax.fori_loop(0, blocks, assemble, 0)
-    whole = nrm[...].reshape(blocks * half, D)
-    for kind in range(2):
-        for quad in range(2):
-            weight[1 + kind, :, quad * 256 : (quad + 1) * 256] = tn(
-                whole, kv[kind, quad].reshape(blocks * half, 256)
-            ).astype(BF)
-    groups[3].begin(1)
-    memory_back.end(3)
-    for part in range(2):
-        dmemory[part * shalf : (part + 1) * shalf, :] = memory_back.result(part)
-    groups[1].advance(7)
-    groups[2].advance(4)
-
-    def spread_back(code):
-        def one(part, carry):
-            s = 2 * cube.other(code) + part
-            total = jnp.zeros((half, D), F32)
-            for kind in range(2):
-                for quad in range(2):
-                    total = total + nt(
-                        kv[kind, quad, s],
-                        ckeys[kind * D : (kind + 1) * D, quad * 256 : (quad + 1) * 256],
-                    )
-            if code == 0:
-                total = total + heard[pl.ds(pl.multiple_of(part * half, half), half), :]
-            nrm[s] = total.astype(BF).reshape(thirds, PIECE, D)
+                    found = cpowers[b, first + third][:, 0:D]
+                    total = total + jnp.where(inside, found.astype(F32), 0.0)
+                if code == 0:
+                    start = pl.multiple_of(part * half + third * PIECE, PIECE)
+                    total = total + heard[pl.ds(start, PIECE), :]
+                nrm[s, third] = total.astype(BF)
             return carry
 
         lax.fori_loop(0, 2, one, 0)
 
     for code in (1, 3, 5, 7):
-        spread_back(code)
-    groups[3].advance(1)
-    rows_back.begin(1)
+        assemble(code)
+    pump("theirs")
     for code in (6, 2, 4, 0):
-        spread_back(code)
-    groups[2].advance(5)
-    for axis in (1, 2):
-        pl.semaphore_wait(ready.at[axis - 1], 1)
-    rows_back.advance(1)
-    groups[3].advance(2)
-    rows_back.advance(2)
-    groups[2].advance(6)
-    groups[3].advance(3)
-    rows_back.end(3)
-    dvec[0:2, :] = jnp.zeros((2, D), F32)
-    dvec[17:VECTORS, :] = jnp.zeros((VECTORS - 17, D), F32)
-    for part in range(2):
-        own_unit, own_spread = centred(own[part].reshape(half, D).astype(F32))
-        dnormed = rows_back.result(part).reshape(half, D)
-        here = pl.ds(part * half, half)
-        dinputs[here, :] = later[here, :] + norm_back(dnormed, own_unit, own_spread, vector(0))
-        dvec[0:1, :] += column_sum(dnormed * own_unit)
-        dvec[1:2, :] += column_sum(dnormed)
-    small.begin(1)
-    groups[3].advance(4)
-    groups[2].advance(7)
-    small.advance(1)
-    groups[3].advance(5)
-    small.advance(2)
-    groups[3].advance(6)
-    small.advance(3)
-    groups[0].end(8)
-    groups[1].end(8)
-    groups[2].end(8)
-    copies = [
+        assemble(code)
+    pump("end")
+    assert not any(counts.values()), counts
+    for turn, first in enumerate((8, 12, 4, 0)):
         pltpu.make_async_copy(
-            weight.at[pl.ds(first, size)], grads.at[pl.ds(first, size)], sem.at[first]
-        )
-        for first, size in ((4, 12), (0, 4))
-    ]
-    copies[0].start()
-    small.end(4)
-    small.take(4)
-    groups[3].advance(7)
-    groups[3].end(8)
-    copies[1].start()
-    for copy in copies:
-        copy.wait()
+            weight.at[pl.ds(first, 4)], grads.at[pl.ds(first, 4)], sem.at[turn]
+        ).wait()
 
 
 def layer_call(sizes, small_ints, own, cot, own_memory, vectors, w_small, w_in, w_out):
@@ -1509,7 +1551,7 @@
             pltpu.VMEM((2, 2, 4, D // 16, D), BF),
             pltpu.VMEM((2, levels - 1, 2, D // 16, D), BF),
             pltpu.VMEM((2, levels - 1, 2, D // 16, D), BF),
-            pltpu.VMEM((3, VECTORS, D), F32),
+            pltpu.VMEM((8, VECTORS, D), F32),
             pltpu.VMEM((levels, VECTORS, D), F32),
             pltpu.SemaphoreType.DMA((16,)),
             pltpu.SemaphoreType.DMA((2, 16)),
@@ -1519,9 +1561,9 @@
             pltpu.SemaphoreType.REGULAR((4, 3)),
             pltpu.SemaphoreType.DMA((2, 14)),
             pltpu.SemaphoreType.DMA((2, 14)),
-            pltpu.SemaphoreType.DMA((6,)),
-            pltpu.SemaphoreType.DMA((6,)),
-            pltpu.SemaphoreType.REGULAR((2,)),
+            pltpu.SemaphoreType.DMA((2, 10)),
+            pltpu.SemaphoreType.DMA((2, 10)),
+            pltpu.SemaphoreType.REGULAR((3,)),
         ],
         compiler_params=pltpu.CompilerParams(
             vmem_limit_bytes=64 << 20, collective_id=0, has_side_effects=True

time: 206 us -> 183 us (0.89)
  Pallas kernels: 201 us -> 178 us
    pallas_call x1, Pallas kernels: 191 us -> 168 us  [layer_call(): pl.pallas_call(body, out_shape=(jax.ShapeDtypeStruct((rows, D), BF), jax....]
where the time goes in v2:
time: 183 us; the launch traced here: 182 us
  Pallas kernels  178 us (97%)
  local copies, waits for them, and re-layouts  3.91 us (2%)
    pallas_call x1, Pallas kernels, layer_call(): pl.pallas_call(body, out_shape=(jax.ShapeDtypeStruct((rows, D), BF), jax....  168 us
    pallas_call x1, Pallas kernels, publish(): pl.pallas_call(publish_kernel, out_shape=tuple([jax.ShapeDtypeStruct(shap...  9.77 us
    unnamed x8, local copies, waits for them, and re-layouts  3.91 us

profile of v2, /device:TPU:0, one launch (start us, length us, event | category | flops | bytes accessed | tf_op | source)
XLA Modules:
  0.0 182.4 jit_solution(7971872226396664956)
XLA Ops:
  0.7 167.8 %shard_map.502 = (bf16[384,512]{1,0:T(8,128)(2,1)}, f32[384,512]{1,0:T(8,128)}, f32[192,512]{1,0:T(8,128)}, f32[24,512]{1,0:T(8,128)}, bf16[16,512,512]{2,1,0:T(8,128)(2,1)}) custom-call(s32[1,33]{1,0:T(1,128)} %refs_0_.1, s32[1,33]{1,0:T(1,128)} %refs_1_.1, s32[1,16]{1,0:T(1,128)} %refs_2_.1, s32[1,16]{1,0:T(1,128)} %refs_3_.1, ...), custom_call_target="tpu_custom_call" | custom-call | tf_op jit(solution)/shard_map/pallas_call | solution.py:1517
  168.5 0.0 copy-start
  168.5 1.1 copy-done
  169.6 0.0 copy-start.1
  169.6 1.0 copy-done.1
  170.6 0.0 copy-start.2
  170.6 1.0 copy-done.2
  171.6 0.0 copy-start.3
  171.6 0.8 copy-done.3
  172.4 9.8 %shard_map.503 = (f32[512,512]{1,0:T(8,128)}, f32[512,512]{1,0:T(8,128)}, f32[512,512]{1,0:T(8,128)}, f32[512,512]{1,0:T(8,128)}, f32[512,512]{1,0:T(8,128)}, /*...) custom-call(bf16[16,512,512]{2,1,0:T(8,128)(2,1)} %get-tuple-element, ...), custom_call_target="tpu_custom_call" | custom-call | tf_op jit(solution)/shard_map/pallas_call | solution.py:904
Async XLA Ops:
  168.5 1.1 copy-start
  169.6 1.0 copy-start.1
  170.6 1.0 copy-start.2
  171.6 0.8 copy-start.3

commit v3 on v2

--- a/solution.py
+++ b/solution.py
@@ -393,21 +393,21 @@
 
 SCHEDULE = dict(
     half="A",
-    heard="BA",
-    pair0="B",
+    feed="AB",
     pair1="A",
-    pair3="AB",
-    sources="BV",
-    middle="CA",
-    self0="CM",
-    self1="BMV",
-    window="AC",
-    self2="B",
-    self3="A",
+    pair2="B",
+    pair3="A",
+    middle="VBCMA",
+    self0="C",
+    self1="M",
+    window="BA",
+    self2="C",
+    self3="AB",
     weights="ECME",
-    through0="BC",
-    theirs="R",
-    end="ECMREACAERBECRSESVECSBE",
+    through0="VB",
+    through1="CE",
+    theirs="BRMVA",
+    end="ECRECERCEBRBASCESES",
 )
 MESH = pl.DeviceIdType.MESH
 PARTS = 2
@@ -486,11 +486,14 @@
 
     def first(c, highest):
         rows = pl.ds(pl.multiple_of(c * chunk, chunk), chunk)
-        place = lax.broadcasted_iota(jnp.int32, (chunk, width), 0) + c * chunk
-        found = jnp.where((place >= low) & (place < high), nt(part_of(keys, c, chunk), queries), NEGATIVE)
+        place = lax.broadcasted_iota(jnp.int32, (chunk, width), 0) - (low - c * chunk)
+        found = jnp.where(
+            place.astype(jnp.uint32) < length, nt(part_of(keys, c, chunk), queries), NEGATIVE
+        )
         scores[rows, :] = found
         return jnp.maximum(highest, jnp.max(found, axis=0, keepdims=True))
 
+    length = (high - low).astype(jnp.uint32)
     highest = lax.fori_loop(0, total // chunk, first, jnp.full((1, width), NEGATIVE, F32))
 
     def second(c, summed):
@@ -553,7 +556,9 @@
             pl.semaphore_signal(
                 barrier, inc=1, device_id={"batch": self.plane(step)}, device_id_type=MESH
             )
-        pl.semaphore_wait(barrier, 6 + self.levels)
+
+    def await_all(self):
+        pl.semaphore_wait(pltpu.get_barrier_semaphore(), 6 + self.levels)
 
     def send(self, code, source, target, send_sem, recv_sem):
         copy = pltpu.make_async_remote_copy(
@@ -844,7 +849,11 @@
             self.take(code, part)
 
     def open(self):
-        for step, part in ((2, 0), (4, 1), (2, 1), (4, 0), (1, 0), (1, 1)):
+        for step, part in ((2, 0), (4, 1), (1, 0), (1, 1)):
+            self.push(step, 0, part)
+
+    def more(self):
+        for step, part in ((2, 1), (4, 0)):
             self.push(step, 0, part)
 
     def pass_on(self):
@@ -870,19 +879,24 @@
 
 
 def publish_kernel(grads, dvec, *refs):
-    kept, outs, (narrow, broad, load_sem, store_sem, keep_sem) = refs[:3], refs[3:-5], refs[-5:]
-    keeps = [pltpu.make_async_copy(kept[i], outs[24 + i], keep_sem.at[i]) for i in range(3)]
+    kept, outs, stages = refs[:3], refs[3:-8], refs[-8:-5]
+    narrow, broad, load_sem, store_sem, keep_sem = refs[-5:]
+    fetches = [pltpu.make_async_copy(kept[i], stages[i], keep_sem.at[i]) for i in range(3)]
+    keeps = [pltpu.make_async_copy(stages[i], outs[24 + i], keep_sem.at[i]) for i in range(3)]
     order = list(range(8, 16)) + list(range(4, 8)) + list(range(4))
     loads = [pltpu.make_async_copy(grads.at[i], narrow.at[i], load_sem.at[i]) for i in order]
-    for load in loads + keeps:
+    ahead = 4
+    for load in loads[:ahead] + fetches:
         load.start()
     for i in range(13):
         outs[10 + i][...] = dvec[i, :]
     for i in range(4):
         outs[23][i * D : (i + 1) * D] = dvec[13 + i, :]
     stores = []
-    for load, i in zip(loads, order):
+    for turn, (load, i) in enumerate(zip(loads, order)):
         load.wait()
+        if turn + ahead < len(loads):
+            loads[turn + ahead].start()
         broad[i] = narrow[i].astype(F32)
         if i < 8:
             target = outs[i]
@@ -893,6 +907,9 @@
         store = pltpu.make_async_copy(broad.at[i], target, store_sem.at[i])
         store.start()
         stores.append(store)
+    for fetch, keep in zip(fetches, keeps):
+        fetch.wait()
+        keep.start()
     for store in stores + keeps:
         store.wait()
 
@@ -909,14 +926,15 @@
         ),
         in_specs=[hbm, vmem] + [hbm] * 3,
         out_specs=tuple([hbm] * 10 + [vmem] * 14 + [hbm] * 3),
-        scratch_shapes=[
+        scratch_shapes=[pltpu.VMEM(array.shape, array.dtype) for array in kept]
+        + [
             pltpu.VMEM((16, D, D), BF),
             pltpu.VMEM((16, D, D), F32),
             pltpu.SemaphoreType.DMA((16,)),
             pltpu.SemaphoreType.DMA((16,)),
             pltpu.SemaphoreType.DMA((3,)),
         ],
-        compiler_params=pltpu.CompilerParams(vmem_limit_bytes=48 << 20),
+        compiler_params=pltpu.CompilerParams(vmem_limit_bytes=64 << 20),
     )(grads, dvec, *kept)
 
 
@@ -926,10 +944,10 @@
     slen,
     tord,
     sord,
-    own,
-    cot,
+    own_far,
+    cot_far,
     own_memory,
-    vectors,
+    vectors_far,
     w_small,
     w_in,
     w_out,
@@ -938,6 +956,9 @@
     dmemory,
     dvec,
     grads,
+    own,
+    cot,
+    vectors,
     vec,
     nrm,
     memory,
@@ -1002,8 +1023,21 @@
     def raw_memory(slot):
         return memory.at[slot]
 
-    gather_rows = Gather(cube, own, raw, send_sem.at[0], recv_sem.at[0])
+    gather_rows = Gather(cube, own_far, raw, send_sem.at[0], recv_sem.at[0])
     gather_sources = Gather(cube, own_memory, raw_memory, send_sem.at[1], recv_sem.at[1])
+    copies = []
+    for index, (source, target) in enumerate(
+        [(own_far, own)]
+        + list(zip(vectors_far, vectors))
+        + [(w_small[i], weight.at[i]) for i in range(8)]
+        + [(w_in.at[:, pl.ds(D * i, D)], weight.at[8 + 2 * i]) for i in range(4)]
+        + [(w_out.at[pl.ds(D * i, D), :], weight.at[9 + 2 * i]) for i in range(4)]
+        + [(cot_far, cot)]
+    ):
+        copy = pltpu.make_async_copy(source, target, sem.at[index])
+        copy.start()
+        copies.append(copy)
+    cube.await_all()
     gather_rows.open()
     def deliver(turn, first):
         def go():
@@ -1072,22 +1106,6 @@
             exchanges[name].advance()
 
     dvec[...] = jnp.zeros((VECTORS, D), F32)
-    row = 0
-    for vector_ref in vectors:
-        for start in range(0, vector_ref.shape[0], D):
-            vec[row : row + 1, :] = vector_ref[start : start + D].astype(F32).reshape(1, D)
-            row += 1
-
-    copies = []
-    for index, (source, target) in enumerate(
-        [(w_small[i], weight.at[i]) for i in range(8)]
-        + [(w_in.at[:, pl.ds(D * i, D)], weight.at[8 + 2 * i]) for i in range(4)]
-        + [(w_out.at[pl.ds(D * i, D), :], weight.at[9 + 2 * i]) for i in range(4)]
-    ):
-        copy = pltpu.make_async_copy(source, target, sem.at[index])
-        copy.start()
-        copies.append(copy)
-
     for order, inverse_of, count in ((tord, tinv, blocks), (sord, sinv, sblocks)):
         for t in range(count):
             found = jnp.int32(0)
@@ -1107,6 +1125,12 @@
 
     for copy in copies:
         copy.wait()
+    gather_rows.more()
+    row = 0
+    for vector_ref in vectors:
+        for start in range(0, vector_ref.shape[0], D):
+            vec[row : row + 1, :] = vector_ref[start : start + D].astype(F32).reshape(1, D)
+            row += 1
 
     states = own[...].reshape(rows, D)
     own_normed = (centred(states.astype(F32))[0] * vector(0) + vector(1)).astype(BF)
@@ -1136,6 +1160,7 @@
     project(1)
     gather_rows.pass_on()
     gather_sources.open()
+    gather_sources.more()
     project(2)
     project(4)
     gather_rows.arrived(3)
@@ -1197,6 +1222,8 @@
             return carry
 
         lax.fori_loop(0, 2, forward, 0)
+        if b == 0:
+            gather_sources.finish()
 
     middle = own[...].reshape(rows, D).astype(F32) + nn(mixed[...].astype(BF), weight[3]) + vector(4)
     found, spread = centred(middle)
@@ -1206,7 +1233,6 @@
     cross_spread = spread
     low[1] = ((nn(low[0], weight[4]) + vector(7)) * scale).astype(BF)
 
-    gather_sources.finish()
     for code in (1, 3, 5, 7):
         gather_sources.arrived(code)
     for part in range(2):
@@ -1512,7 +1538,11 @@
     def body(*refs):
         head, rest = refs[:7], refs[7:]
         vector_refs, rest = rest[:count], rest[count:]
-        layer_kernel(sizes, *head, vector_refs, rest[:8], *rest[8:])
+        scratch = rest[17:]
+        layer_kernel(
+            sizes, *head, vector_refs, rest[:8], *rest[8:15],
+            *rest[15:17], scratch[:count], *scratch[count:],
+        )
 
     return pl.pallas_call(
         body,
@@ -1523,9 +1553,11 @@
             jax.ShapeDtypeStruct((VECTORS, D), F32),
             jax.ShapeDtypeStruct((16, D, D), BF),
         ),
-        in_specs=[smem] * 4 + [vmem] * (3 + count) + [hbm] * 10,
+        in_specs=[smem] * 4 + [hbm] * 2 + [vmem] + [hbm] * (count + 10),
         out_specs=(vmem, vmem, vmem, vmem, hbm),
-        scratch_shapes=[
+        scratch_shapes=[pltpu.VMEM(own.shape, BF), pltpu.VMEM(cot.shape, BF)]
+        + [pltpu.VMEM(vector.shape, BF) for vector in vectors]
+        + [
             pltpu.VMEM((VECTORS, D), F32),
             pltpu.VMEM((blocks, half // PIECE, PIECE, D), BF),
             pltpu.VMEM((sblocks, shalf, D), BF),
@@ -1553,7 +1585,7 @@
             pltpu.VMEM((2, levels - 1, 2, D // 16, D), BF),
             pltpu.VMEM((8, VECTORS, D), F32),
             pltpu.VMEM((levels, VECTORS, D), F32),
-            pltpu.SemaphoreType.DMA((16,)),
+            pltpu.SemaphoreType.DMA((32,)),
             pltpu.SemaphoreType.DMA((2, 16)),
             pltpu.SemaphoreType.DMA((2, 16)),
             pltpu.SemaphoreType.DMA((4, 22)),

time: 183 us -> 176 us (0.962)
  local copies, waits for them, and re-layouts: 3.91 us -> 0 us
  Pallas kernels: 178 us -> 175 us
    pallas_call x1, Pallas kernels: 168 us -> 163 us  [layer_call(): pl.pallas_call(body, out_shape=(jax.ShapeDtypeStruct((rows, D), BF), jax....]
    unnamed x8 -> x0, local copies, waits for them, and re-layouts: 3.91 us -> none
    pallas_call x1, Pallas kernels: 9.77 us -> 11.7 us  [publish(): pl.pallas_call(publish_kernel, out_shape=tuple([jax.ShapeDtypeStruct(shap...]
where the time goes in v3:
time: 176 us
  Pallas kernels  175 us (99%)
    pallas_call x1, Pallas kernels, layer_call(): pl.pallas_call(body, out_shape=(jax.ShapeDtypeStruct((rows, D), BF), jax....  163 us
    pallas_call x1, Pallas kernels, publish(): pl.pallas_call(publish_kernel, out_shape=tuple([jax.ShapeDtypeStruct(shap...  11.7 us

profile of v3, /device:TPU:0, one launch (start us, length us, event | category | flops | bytes accessed | tf_op | source)
XLA Modules:
  0.0 175.7 jit_solution(5997102787887099561)
XLA Ops:
  0.7 163.1 %shard_map.502 = (bf16[384,512]{1,0:T(8,128)(2,1)}, f32[384,512]{1,0:T(8,128)}, f32[192,512]{1,0:T(8,128)}, f32[24,512]{1,0:T(8,128)}, bf16[16,512,512]{2,1,0:T(8,128)(2,1)}) custom-call(s32[1,33]{1,0:T(1,128)} %refs_0_.1, s32[1,33]{1,0:T(1,128)} %refs_1_.1, s32[1,16]{1,0:T(1,128)} %refs_2_.1, s32[1,16]{1,0:T(1,128)} %refs_3_.1, ...), custom_call_target="tpu_custom_call" | custom-call | tf_op jit(solution)/shard_map/pallas_call | solution.py:1547
  163.8 11.7 %shard_map.503 = (f32[512,512]{1,0:T(8,128)}, f32[512,512]{1,0:T(8,128)}, f32[512,512]{1,0:T(8,128)}, f32[512,512]{1,0:T(8,128)}, f32[512,512]{1,0:T(8,128)}, /*...) custom-call(bf16[16,512,512]{2,1,0:T(8,128)(2,1)} %get-tuple-element, ...), custom_call_target="tpu_custom_call" | custom-call | tf_op jit(solution)/shard_map/pallas_call | solution.py:921

commit v4 on v3

--- a/solution.py
+++ b/solution.py
@@ -391,23 +391,24 @@
 CHUNK = 256
 PIECE = 64
 
+GROUPS = ((8, 4), (12, 4), (3, 5), (0, 3))
 SCHEDULE = dict(
     half="A",
-    feed="AB",
-    pair1="A",
-    pair2="B",
+    feed="A",
+    heard="B",
+    pair1="AB",
     pair3="A",
-    middle="VBCMA",
-    self0="C",
-    self1="M",
-    window="BA",
-    self2="C",
-    self3="AB",
-    weights="ECME",
-    through0="VB",
-    through1="CE",
-    theirs="BRMVA",
-    end="ECRECERCEBRBASCESES",
+    sums="V",
+    sources="MB",
+    middle="ACM",
+    self0="CB",
+    window="AM",
+    self2="BCA",
+    weights="CEB",
+    through0="EA",
+    through1="BA",
+    theirs="RV",
+    end="CEREVCRBECRESBEMCSCESE",
 )
 MESH = pl.DeviceIdType.MESH
 PARTS = 2
@@ -612,9 +613,9 @@
 class Reduce(Steps):
     last = 8
 
-    def __init__(self, cube, panels, first, pair, flat, edge, deep, leave, send_sem, recv_sem, sent, before, finish):
+    def __init__(self, cube, panels, first, count, pair, flat, edge, deep, leave, send_sem, recv_sem, sent, before, finish):
         self.before, self.finish, self.freed = before, finish, set()
-        self.cube, self.panels, self.first = cube, panels, first
+        self.cube, self.panels, self.first, self.count = cube, panels, first, count
         self.pair, self.flat, self.edge, self.deep, self.leave = pair, flat, edge, deep, leave
         self.send_sem, self.recv_sem, self.sent = send_sem, recv_sem, sent
 
@@ -631,9 +632,8 @@
                 self.before.await_free(index)
         if step == 4:
             for k in range(1, self.cube.levels):
-                there = self.first + self.cube.plane(k)
                 for axis in (1, 2):
-                    self.leave[k - 1, axis - 1] = self.panels[there, self.rows(axis=axis, further=0), :]
+                    self.leave[k - 1, axis - 1] = self.share(self.cube.plane(k), axis)[...]
         super().begin(step)
 
     def rows(self, core=0, axis=None, far=0, further=None):
@@ -649,7 +649,12 @@
         return pl.ds(pl.multiple_of(start, D // 16), size)
 
     def all(self, rows):
-        return self.panels.at[pl.ds(self.first, 4), rows, :]
+        return self.panels.at[pl.ds(self.first, self.count), rows, :]
+
+    def share(self, plane, axis):
+        width = D // self.cube.levels
+        lanes = pl.ds(pl.multiple_of(plane * width, width), width)
+        return self.panels.at[pl.ds(self.first, self.count), self.rows(axis=axis, further=0), lanes]
 
     def moves(self, step):
         cube = self.cube
@@ -683,12 +688,11 @@
                 for axis in (1, 2)
             ]
         if step == 5:
-            there = self.first + cube.level
             return [
                 (
                     {"batch": cube.plane(k)},
-                    self.panels.at[there, self.rows(axis=axis, further=0), :],
-                    self.panels.at[there, self.rows(axis=axis, further=0), :],
+                    self.share(cube.level, axis),
+                    self.share(cube.level, axis),
                     9 + 2 * k + axis - 1,
                 )
                 for k in range(1, cube.levels)
@@ -709,7 +713,7 @@
             self.panels[there, rows, :] = total.astype(BF)
             return carry
 
-        lax.fori_loop(0, 4, one, 0)
+        lax.fori_loop(0, self.count, one, 0)
 
     def take(self, step):
         if step == 1:
@@ -721,13 +725,12 @@
             for axis in (1, 2):
                 self.add(self.rows(axis=axis, further=0), self.edge.at[axis - 1])
         elif step == 4:
-            there = self.first + self.cube.level
             for axis in (1, 2):
-                rows = self.rows(axis=axis, further=0)
-                total = self.panels[there, rows, :].astype(F32)
+                here = self.share(self.cube.level, axis)
+                total = here[...].astype(F32)
                 for k in range(self.cube.levels - 1):
                     total = total + self.deep[k, axis - 1].astype(F32)
-                self.panels[there, rows, :] = total.astype(BF)
+                here[...] = total.astype(BF)
         elif step == 8:
             self.finish()
         for index in {1: (0,), 3: (1, 2)}.get(step, ()):
@@ -885,7 +888,7 @@
     keeps = [pltpu.make_async_copy(stages[i], outs[24 + i], keep_sem.at[i]) for i in range(3)]
     order = list(range(8, 16)) + list(range(4, 8)) + list(range(4))
     loads = [pltpu.make_async_copy(grads.at[i], narrow.at[i], load_sem.at[i]) for i in order]
-    ahead = 4
+    ahead = 16
     for load in loads[:ahead] + fetches:
         load.start()
     for i in range(13):
@@ -1039,21 +1042,24 @@
         copies.append(copy)
     cube.await_all()
     gather_rows.open()
-    def deliver(turn, first):
+    def deliver(turn, first, count):
         def go():
             pltpu.make_async_copy(
-                weight.at[pl.ds(first, 4)], grads.at[pl.ds(first, 4)], sem.at[turn]
+                weight.at[pl.ds(first, count)], grads.at[pl.ds(first, count)], sem.at[turn]
             ).start()
 
         return go
 
     groups = []
-    for turn, first in enumerate((8, 12, 4, 0)):
+    for turn, (first, count) in enumerate(GROUPS):
+        side = turn % 2
+        some = pl.ds(0, count)
         groups.append(
             Reduce(
-                cube, weight, first, pairs.at[turn % 2], flats.at[turn % 2], edges.at[turn % 2],
-                deeps.at[turn % 2], leaves.at[turn % 2], group_send.at[turn], group_recv.at[turn],
-                group_sent.at[turn], groups[turn - 2] if turn > 1 else None, deliver(turn, first),
+                cube, weight, first, count, pairs.at[side, some], flats.at[side, :, some],
+                edges.at[side, :, some], deeps.at[side, :, :, some], leaves.at[side, :, :, some],
+                group_send.at[turn], group_recv.at[turn], group_sent.at[turn],
+                groups[turn - 2] if turn > 1 else None, deliver(turn, first, count),
             )
         )
 
@@ -1512,9 +1518,9 @@
         assemble(code)
     pump("end")
     assert not any(counts.values()), counts
-    for turn, first in enumerate((8, 12, 4, 0)):
+    for turn, (first, count) in enumerate(GROUPS):
         pltpu.make_async_copy(
-            weight.at[pl.ds(first, 4)], grads.at[pl.ds(first, 4)], sem.at[turn]
+            weight.at[pl.ds(first, count)], grads.at[pl.ds(first, count)], sem.at[turn]
         ).wait()
 
 
@@ -1529,6 +1535,7 @@
     )
     sources = sblocks * shalf
     levels = sizes["levels"]
+    most = max(count for _, count in GROUPS)
     vmem = pl.BlockSpec(memory_space=pltpu.VMEM)
     smem = pl.BlockSpec(memory_space=pltpu.SMEM)
     hbm = pl.BlockSpec(memory_space=pl.ANY)
@@ -1578,11 +1585,11 @@
             pltpu.VMEM((3, rows, D), BF),
             pltpu.SMEM((blocks,), jnp.int32),
             pltpu.SMEM((sblocks,), jnp.int32),
-            pltpu.VMEM((2, 4, D // 2, D), BF),
-            pltpu.VMEM((2, 2, 4, D // 8, D), BF),
-            pltpu.VMEM((2, 2, 4, D // 16, D), BF),
-            pltpu.VMEM((2, levels - 1, 2, D // 16, D), BF),
-            pltpu.VMEM((2, levels - 1, 2, D // 16, D), BF),
+            pltpu.VMEM((2, most, D // 2, D), BF),
+            pltpu.VMEM((2, 2, most, D // 8, D), BF),
+            pltpu.VMEM((2, 2, most, D // 16, D), BF),
+            pltpu.VMEM((2, levels - 1, 2, most, D // 16, D // levels), BF),
+            pltpu.VMEM((2, levels - 1, 2, most, D // 16, D // levels), BF),
             pltpu.VMEM((8, VECTORS, D), F32),
             pltpu.VMEM((levels, VECTORS, D), F32),
             pltpu.SemaphoreType.DMA((32,)),

time: 176 us -> 172 us (0.977)
  Pallas kernels: 175 us -> 171 us
    pallas_call x1, Pallas kernels: 163 us -> 160 us  [layer_call(): pl.pallas_call(body, out_shape=(jax.ShapeDtypeStruct((rows, D), BF), jax....]
where the time goes in v4:
time: 172 us
  Pallas kernels  171 us (99%)
    pallas_call x1, Pallas kernels, layer_call(): pl.pallas_call(body, out_shape=(jax.ShapeDtypeStruct((rows, D), BF), jax....  160 us
    pallas_call x1, Pallas kernels, publish(): pl.pallas_call(publish_kernel, out_shape=tuple([jax.ShapeDtypeStruct(shap...  11 us

profile of v4, /device:TPU:0, one launch (start us, length us, event | category | flops | bytes accessed | tf_op | source)
XLA Modules:
  0.0 172.1 jit_solution(8694694844314852463)
XLA Ops:
  0.7 160.3 %shard_map.502 = (bf16[384,512]{1,0:T(8,128)(2,1)}, f32[384,512]{1,0:T(8,128)}, f32[192,512]{1,0:T(8,128)}, f32[24,512]{1,0:T(8,128)}, bf16[16,512,512]{2,1,0:T(8,128)(2,1)}) custom-call(s32[1,33]{1,0:T(1,128)} %refs_0_.1, s32[1,33]{1,0:T(1,128)} %refs_1_.1, s32[1,16]{1,0:T(1,128)} %refs_2_.1, s32[1,16]{1,0:T(1,128)} %refs_3_.1, ...), custom_call_target="tpu_custom_call" | custom-call | tf_op jit(solution)/shard_map/pallas_call | solution.py:1554
  160.9 11.0 %shard_map.503 = (f32[512,512]{1,0:T(8,128)}, f32[512,512]{1,0:T(8,128)}, f32[512,512]{1,0:T(8,128)}, f32[512,512]{1,0:T(8,128)}, f32[512,512]{1,0:T(8,128)}, /*...) custom-call(bf16[16,512,512]{2,1,0:T(8,128)(2,1)} %get-tuple-element, ...), custom_call_target="tpu_custom_call" | custom-call | tf_op jit(solution)/shard_map/pallas_call | solution.py:924

commit v5 on v4

--- a/solution.py
+++ b/solution.py
@@ -1131,13 +1131,13 @@
 
     for copy in copies:
         copy.wait()
-    gather_rows.more()
     row = 0
     for vector_ref in vectors:
         for start in range(0, vector_ref.shape[0], D):
             vec[row : row + 1, :] = vector_ref[start : start + D].astype(F32).reshape(1, D)
             row += 1
 
+    gather_rows.more()
     states = own[...].reshape(rows, D)
     own_normed = (centred(states.astype(F32))[0] * vector(0) + vector(1)).astype(BF)
     queries[...] = ((nn(own_normed, weight[0]) + vector(2)) * scale).astype(BF)
@@ -1162,6 +1162,29 @@
 
     for part in range(2):
         project_block(2 * me + part, own[part].reshape(half, D))
+    def limits(b):
+        index = lax.broadcasted_iota(jnp.int32, (1, 4 * half), 1)
+        row = index
+        for h in range(1, 4):
+            row = jnp.where(index >= h * half, index - h * half, row)
+        position = base[b] * half + row
+        start = jnp.zeros_like(position)
+        for end in tends:
+            start = jnp.where(position >= end, end, start)
+        shift = (base[b] + 1) * half - window
+        return start - shift, position - shift + 1
+
+    bounds = [limits(b) for b in range(2)]
+    index = lax.broadcasted_iota(jnp.int32, (1, 2 * rows), 1)
+    row = jnp.where(index >= rows, index - rows, index)
+    position = jnp.where(row >= half, base[1] * half + row - half, base[0] * half + row)
+    cross_begin = jnp.zeros_like(position)
+    cross_stop = jnp.full_like(position, sources)
+    for end, send in zip(tends, sends):
+        cross_begin = jnp.where(position >= end, send, cross_begin)
+    for end, send in reversed(list(zip(tends, sends))):
+        cross_stop = jnp.where(position < end, send, cross_stop)
+
     gather_rows.arrived(1)
     project(1)
     gather_rows.pass_on()
@@ -1180,18 +1203,6 @@
     gather_rows.close()
     gather_sources.pass_on()
 
-    def limits(b):
-        index = lax.broadcasted_iota(jnp.int32, (1, 4 * half), 1)
-        row = index
-        for h in range(1, 4):
-            row = jnp.where(index >= h * half, index - h * half, row)
-        position = base[b] * half + row
-        start = jnp.zeros_like(position)
-        for end in tends:
-            start = jnp.where(position >= end, end, start)
-        shift = (base[b] + 1) * half - window
-        return start - shift, position - shift + 1
-
     kwin, vwin = [
         cpowers.at[kind, pl.ds(0, window // PIECE), :, pl.ds(D, 4 * HDIM)] for kind in range(2)
     ]
@@ -1208,7 +1219,7 @@
                     target[j * thirds - skip : (j + 1) * thirds - skip] = block
 
     for b in range(2):
-        begin, stop = limits(b)
+        begin, stop = bounds[b]
 
         def forward(quad, carry, b=b, begin=begin, stop=stop):
             fill(b, quad)
@@ -1261,24 +1272,14 @@
         return carry
 
     lax.fori_loop(0, sources // step, sources_of, 0)
-    index = lax.broadcasted_iota(jnp.int32, (1, 2 * rows), 1)
-    row = jnp.where(index >= rows, index - rows, index)
-    position = jnp.where(row >= half, base[1] * half + row - half, base[0] * half + row)
-    begin = jnp.zeros_like(position)
-    stop = jnp.full_like(position, sources)
-    for end, send in zip(tends, sends):
-        begin = jnp.where(position >= end, send, begin)
-    for end, send in reversed(list(zip(tends, sends))):
-        stop = jnp.where(position < end, send, stop)
-
     def cross_forward(pair, carry):
         lanes = pl.ds(pl.multiple_of(pair * 128, 128), 128)
         out, inverse = attend(
             spread_heads(low[1, :, lanes].astype(F32), 2).astype(BF),
             ckeys.at[:, lanes],
             cvalues.at[:, lanes],
-            begin,
-            stop,
+            cross_begin,
+            cross_stop,
             scores,
             cpowers.at[pair],
         )

time: 172 us -> 172 us (level)
  no operation moved by 1% of the time
where the time goes in v5:
time: 172 us
  Pallas kernels  171 us (99%)
    pallas_call x1, Pallas kernels, layer_call(): pl.pallas_call(body, out_shape=(jax.ShapeDtypeStruct((rows, D), BF), jax....  160 us
    pallas_call x1, Pallas kernels, publish(): pl.pallas_call(publish_kernel, out_shape=tuple([jax.ShapeDtypeStruct(shap...  11 us

profile of v5, /device:TPU:0, one launch (start us, length us, event | category | flops | bytes accessed | tf_op | source)
XLA Modules:
  0.0 172.0 jit_solution(2443193709020973558)
XLA Ops:
  0.7 160.1 %shard_map.502 = (bf16[384,512]{1,0:T(8,128)(2,1)}, f32[384,512]{1,0:T(8,128)}, f32[192,512]{1,0:T(8,128)}, f32[24,512]{1,0:T(8,128)}, bf16[16,512,512]{2,1,0:T(8,128)(2,1)}) custom-call(s32[1,33]{1,0:T(1,128)} %refs_0_.1, s32[1,33]{1,0:T(1,128)} %refs_1_.1, s32[1,16]{1,0:T(1,128)} %refs_2_.1, s32[1,16]{1,0:T(1,128)} %refs_3_.1, ...), custom_call_target="tpu_custom_call" | custom-call | tf_op jit(solution)/shard_map/pallas_call | solution.py:1555
  160.8 11.0 %shard_map.503 = (f32[512,512]{1,0:T(8,128)}, f32[512,512]{1,0:T(8,128)}, f32[512,512]{1,0:T(8,128)}, f32[512,512]{1,0:T(8,128)}, f32[512,512]{1,0:T(8,128)}, /*...) custom-call(bf16[16,512,512]{2,1,0:T(8,128)(2,1)} %get-tuple-element, ...), custom_call_target="tpu_custom_call" | custom-call | tf_op jit(solution)/shard_map/pallas_call | solution.py:924
